TPU v7x, 32 devices: a whole 2x2x4 slice. The times are simulated.
32 devices in a mesh: dp: 16 (over z, y, core), mp: 2 (over x).
Axes of the slice: x: 2, y: 2, z: 4, core: 2. Of those that a mesh axis runs over, the one named last changes fastest.
Arguments:
- inputs: bfloat16 [64, 512, 768], P('dp', 'mp'), may hold values from -6 to 6
- segment_ids: int32 [64, 512], P('dp'), may hold values from 0 to 15, as said below
- ln1_gain: bfloat16 [768], replicated, may hold values from 0.099609375 to 1.8984375
- ln1_bias: bfloat16 [768], replicated, may hold values from -0.3984375 to 0.3984375
- value_weight: bfloat16 [768, 768], replicated, may hold values from -0.21875 to 0.21875
- value_bias: bfloat16 [768], replicated, may hold values from -0.5 to 0.5
- random_logits: bfloat16 [12, 512, 512], P(None, 'mp'), may hold values from -8 to 8
- out_weight: bfloat16 [768, 768], replicated, may hold values from -0.875 to 0.875
- out_bias: bfloat16 [768], replicated, may hold values from -0.5 to 0.5
- ln2_gain: bfloat16 [768], replicated, may hold values from 0.099609375 to 1.8984375
- ln2_bias: bfloat16 [768], replicated, may hold values from -0.3984375 to 0.3984375
- up_weight: bfloat16 [768, 3072], P(None, 'mp'), may hold values from -0.21875 to 0.21875
- up_bias: bfloat16 [3072], P('mp'), may hold values from -0.5 to 0.5
- down_weight: bfloat16 [3072, 768], P('mp'), may hold values from -0.109375 to 0.109375
- down_bias: bfloat16 [768], replicated, may hold values from -0.5 to 0.5
- out_cotangent: bfloat16 [64, 512, 768], P('dp', 'mp'), may hold values from -6 to 6
Outputs:
- layer_out: bfloat16 [64, 512, 768], P('dp', 'mp')
- grad_inputs: float32 [64, 512, 768], P('dp', 'mp')
- grad_ln1_gain: float32 [768], P(('dp', 'mp'))
- grad_ln1_bias: float32 [768], P(('dp', 'mp'))
- grad_value_weight: float32 [768, 768], P(('dp', 'mp'))
- grad_value_bias: float32 [768], P(('dp', 'mp'))
- grad_random_logits: float32 [12, 512, 512], P(None, 'mp', 'dp')
- grad_out_weight: float32 [768, 768], P(('dp', 'mp'))
- grad_out_bias: float32 [768], P(('dp', 'mp'))
- grad_ln2_gain: float32 [768], P(('dp', 'mp'))
- grad_ln2_bias: float32 [768], P(('dp', 'mp'))
- grad_up_weight: float32 [768, 3072], P('dp', 'mp')
- grad_up_bias: float32 [2, 1536], P('mp', 'dp')
- grad_down_weight: float32 [3072, 768], P('mp', 'dp')
- grad_down_bias: float32 [768], P(('dp', 'mp'))
Inputs may be any that keep to these rules, and one draw needn't show every extreme that they name: `segment_ids`: in each row the ids start at 0 and never fall; of the 4 rows of each index of dp, one row is a single document, and another reaches the largest id.
All inputs are finite; a program needn't handle non-finite values.
Results may differ from a plain program's by a relative error of at most 0.015.
Values may be sent and summed in bfloat16 or wider, within the bound.
No kernel may reach another device: no remote copies, remote signals or barrier semaphores. Data moves between devices by JAX's collectives and lax.ppermute only.
A program may use at most 192 MiB of HBM per device.

v0:
```python
import jax
import jax.numpy as jnp
from jax import lax
from jax.sharding import PartitionSpec as P


def smooth(t):
    return jax.nn.gelu(t, approximate=True)


def contract_rows(left, right):
    return lax.dot_general(
        left, right, (((0,), (0,)), ((), ())), preferred_element_type=jnp.float32
    )


def contract_cols(left, right):
    return lax.dot_general(
        left, right, (((1,), (1,)), ((), ())), preferred_element_type=jnp.float32
    )


def normalize(x, gain, shift):
    centred = x - jnp.mean(x, -1, keepdims=True)
    scale = lax.rsqrt(jnp.mean(centred * centred, -1, keepdims=True) + 1e-05)
    unit = centred * scale
    return (unit * gain + shift, unit, scale)


def normalize_back(grad, unit, scale, gain):
    scaled = grad * gain
    inner = scale * (
        scaled
        - jnp.mean(scaled, -1, keepdims=True)
        - unit * jnp.mean(scaled * unit, -1, keepdims=True)
    )
    return (inner, jnp.sum(grad * unit, 0), jnp.sum(grad, 0))


def shards(
    inputs,
    segment_ids,
    ln1_gain,
    ln1_bias,
    value_weight,
    value_bias,
    random_logits,
    out_weight,
    out_bias,
    ln2_gain,
    ln2_bias,
    up_weight,
    up_bias,
    down_weight,
    down_bias,
    out_cotangent,
):
    seqs, local_len, width = inputs.shape
    heads = random_logits.shape[0]
    full_len = segment_ids.shape[1]
    head_dim = width // heads
    rows = seqs * local_len
    gain_one = ln1_gain.astype(jnp.float32)
    gain_two = ln2_gain.astype(jnp.float32)
    start_x = inputs.astype(jnp.float32).reshape(rows, width)
    normed_one, unit_one, scale_one = normalize(start_x, gain_one, ln1_bias.astype(jnp.float32))
    h1_low = normed_one.astype(jnp.bfloat16)
    values = (
        jnp.dot(h1_low, value_weight, preferred_element_type=jnp.float32)
        + value_bias.astype(jnp.float32)
    ).astype(jnp.bfloat16)
    gathered = lax.all_gather(values.reshape(seqs, local_len, width), "mp", axis=1, tiled=True)
    every_head = gathered.reshape(seqs, full_len, heads, head_dim)
    offset = lax.axis_index("mp") * local_len
    own_segs = lax.dynamic_slice_in_dim(segment_ids, offset, local_len, 1)
    same = own_segs[:, :, None] == segment_ids[:, None, :]
    scores = jnp.where(same[:, None], random_logits.astype(jnp.float32)[None], -1e30)
    peak = jnp.max(scores, -1, keepdims=True)
    expo = jnp.exp(scores - peak)
    total = jnp.sum(expo, -1, keepdims=True)
    probs = expo / total
    probs_low = probs.astype(jnp.bfloat16)
    mixed = jnp.einsum("shqk,skhd->sqhd", probs_low, every_head, preferred_element_type=jnp.float32)
    mixed_low = mixed.reshape(rows, width).astype(jnp.bfloat16)
    resid = (
        start_x
        + jnp.dot(mixed_low, out_weight, preferred_element_type=jnp.float32)
        + out_bias.astype(jnp.float32)
    )
    normed_two, unit_two, scale_two = normalize(resid, gain_two, ln2_bias.astype(jnp.float32))
    h2_low = normed_two.astype(jnp.bfloat16)
    grad_low = out_cotangent.reshape(rows, width)
    h2_full = lax.all_gather(
        h2_low.reshape(seqs, local_len, width), "mp", axis=1, tiled=True
    ).reshape(seqs * full_len, width)
    pre = jnp.dot(h2_full, up_weight, preferred_element_type=jnp.float32) + up_bias.astype(
        jnp.float32
    )
    act, gelu_pull = jax.vjp(smooth, pre)
    act_low = act.astype(jnp.bfloat16)
    partial_out = jnp.dot(act_low, down_weight, preferred_element_type=jnp.float32).reshape(
        seqs, full_len, width
    )
    ffn_out = lax.psum_scatter(
        partial_out.astype(jnp.bfloat16), "mp", scatter_dimension=1, tiled=True
    ).astype(jnp.float32).reshape(rows, width) + down_bias.astype(jnp.float32)
    final = resid + ffn_out
    grad_full = lax.all_gather(out_cotangent, "mp", axis=1, tiled=True).reshape(
        seqs * full_len, width
    )
    grad_down = contract_rows(act_low, grad_full)
    grad_act = contract_cols(grad_full, down_weight)
    grad_pre = gelu_pull(grad_act)[0].astype(jnp.bfloat16)
    grad_up_b = jnp.sum(grad_pre.astype(jnp.float32), 0)
    grad_up = contract_rows(h2_full, grad_pre)
    h2_terms = contract_cols(grad_pre, up_weight).reshape(seqs, full_len, width)
    grad_h2 = (
        lax.psum_scatter(h2_terms.astype(jnp.bfloat16), "mp", scatter_dimension=1, tiled=True)
        .astype(jnp.float32)
        .reshape(rows, width)
    )
    grad_final = grad_low.astype(jnp.float32)
    grad_down_b = jnp.sum(grad_final, 0)
    inner_two, gain_two_grad, shift_two_grad = normalize_back(
        grad_h2, unit_two, scale_two, gain_two
    )
    grad_resid = grad_final + inner_two
    grad_o_low = grad_resid.astype(jnp.bfloat16)
    grad_out_b = jnp.sum(grad_o_low.astype(jnp.float32), 0)
    grad_out_w = contract_rows(mixed_low, grad_o_low)
    grad_mixed = (
        contract_cols(grad_o_low, out_weight)
        .astype(jnp.bfloat16)
        .reshape(seqs, local_len, heads, head_dim)
    )
    grad_probs = jnp.einsum(
        "sqhd,skhd->shqk", grad_mixed, every_head, preferred_element_type=jnp.float32
    )
    grad_scores = probs * (grad_probs - jnp.sum(probs * grad_probs, -1, keepdims=True))
    grad_logits = jnp.sum(grad_scores, 0)
    value_terms = jnp.einsum(
        "shqk,sqhd->skhd", probs_low, grad_mixed, preferred_element_type=jnp.float32
    ).reshape(seqs, full_len, width)
    grad_values = (
        lax.psum_scatter(value_terms.astype(jnp.bfloat16), "mp", scatter_dimension=1, tiled=True)
        .astype(jnp.float32)
        .reshape(rows, width)
        .astype(jnp.bfloat16)
    )
    grad_value_b = jnp.sum(grad_values.astype(jnp.float32), 0)
    grad_value_w = contract_rows(h1_low, grad_values)
    inner_one, gain_one_grad, shift_one_grad = normalize_back(
        contract_cols(grad_values, value_weight), unit_one, scale_one, gain_one
    )
    grad_x = (grad_resid + inner_one).reshape(seqs, local_len, width)
    vectors = jnp.stack(
        [
            gain_one_grad,
            shift_one_grad,
            grad_value_b,
            grad_out_b,
            gain_two_grad,
            shift_two_grad,
            grad_down_b,
        ]
    )
    value_w_part, out_w_part, vector_part = (
        lax.psum_scatter(grad_value_w, ("dp", "mp"), scatter_dimension=0, tiled=True),
        lax.psum_scatter(grad_out_w, ("dp", "mp"), scatter_dimension=0, tiled=True),
        lax.psum_scatter(vectors, ("dp", "mp"), scatter_dimension=1, tiled=True),
    )
    up_part, up_b_part, down_part, logit_part = (
        lax.psum_scatter(
            grad_up.astype(jnp.bfloat16), "dp", scatter_dimension=0, tiled=True
        ).astype(jnp.float32),
        lax.psum_scatter(
            grad_up_b[None].astype(jnp.bfloat16), "dp", scatter_dimension=1, tiled=True
        ).astype(jnp.float32),
        lax.psum_scatter(
            grad_down.astype(jnp.bfloat16), "dp", scatter_dimension=1, tiled=True
        ).astype(jnp.float32),
        lax.psum_scatter(
            grad_logits.astype(jnp.bfloat16), "dp", scatter_dimension=2, tiled=True
        ).astype(jnp.float32),
    )
    return (
        final.astype(jnp.bfloat16).reshape(seqs, local_len, width),
        grad_x,
        vector_part[0],
        vector_part[1],
        value_w_part,
        vector_part[2],
        logit_part,
        out_w_part,
        vector_part[3],
        vector_part[4],
        vector_part[5],
        up_part,
        up_b_part,
        down_part,
        vector_part[6],
    )


def solution(mesh):
    in_specs = (
        P("dp", "mp", None),
        P("dp", None),
        P(),
        P(),
        P(),
        P(),
        P(None, "mp", None),
        P(),
        P(),
        P(),
        P(),
        P(None, "mp"),
        P("mp"),
        P("mp", None),
        P(),
        P("dp", "mp", None),
    )
    out_specs = (
        P("dp", "mp", None),
        P("dp", "mp", None),
        P(("dp", "mp")),
        P(("dp", "mp")),
        P(("dp", "mp"), None),
        P(("dp", "mp")),
        P(None, "mp", "dp"),
        P(("dp", "mp"), None),
        P(("dp", "mp")),
        P(("dp", "mp")),
        P(("dp", "mp")),
        P("dp", "mp"),
        P("mp", "dp"),
        P("mp", "dp"),
        P(("dp", "mp")),
    )
    return jax.shard_map(shards, mesh=mesh, in_specs=in_specs, out_specs=out_specs, check_vma=False)
```

profile of v0, /device:TPU:0, one launch (start us, length us, event | category | flops | bytes accessed | tf_op | source)
XLA Modules:
  0.0 893.9 jit_solution(10221537761894723462)
XLA Ops:
  9.6 1.8 convert_reduce_fusion.1
  11.4 2.0 fusion.33
  14.7 2.6 add_convert_fusion.1
  17.4 5.3 convert_element_type.157
  23.1 18.7 %fusion.6 = (f32[4,12,256]{2,1,0:T(8,128)S(1)}, f32[4,12,256,512]{3,2,1,0:T(8,128)}) fusion(f32[12,256,512]{2,1,0:T(8,128)} %convert_element_type.157, pred[4,256,512]{2,1,0:T(8,128)(4,1)S(1)} %broadcast_compare_fusion), kind=kOutput, calls=%fused_computation.10 | output fusion | flops 25166336 | bytes 32030720 | tf_op jit(solution)/shard_map/sub | solution.py:79
  41.8 23.2 %all-gather.4.cloned.1.call-done = bf16[4,512,768]{2,1,0:T(8,128)(2,1)} async-done(((bf16[4,256,768]{2,1,0:T(8,128)(2,1)}), bf16[4,512,768]{2,1,0:T(8,128)(2,1)}) %all-gather.4.cloned.1.call-update) | async-done | bytes 3145744 | tf_op jit(solution)/shard_map/all_gather | solution.py:72
  65.1 4.9 copy.51
  70.0 40.2 %fusion.61 = bf16[4,256,12,64]{1,3,2,0:T(8,128)(2,1)} fusion(bf16[4,512,12,64]{1,3,2,0:T(8,128)(2,1)} %bitcast.131, f32[4,12,256]{2,1,0:T(8,128)S(1)} %get-tuple-element.67, f32[12,256,512]{2,1,0:T(8,128)} %convert_element_type.157, pred[4,256,512]{2,1,0:T(8,128)(4,1)S(1)} %broadcast_compare_fusion), kind=kOutput, calls=%fused_computation.85 | convolution fusion | flops 837562880 | bytes 11583488 | tf_op jit(solution)/shard_map/shqk,skhd->sqhd/dot_general | solution.py:83
  110.2 2.8 copy.52
  113.4 1.7 fusion.89
  115.7 1.7 add_convert_fusion
  118.2 44.3 %all-gather.6.cloned.1.call-done = bf16[4,512,768]{2,1,0:T(8,128)(2,1)} async-done(((bf16[4,256,768]{2,1,0:T(8,128)(2,1)}), bf16[4,512,768]{2,1,0:T(8,128)(2,1)}) %all-gather.6.cloned.1.call-update) | async-done | bytes 3145744 | tf_op jit(solution)/shard_map/all_gather | solution.py:93
  162.5 13.4 %multiply_convert_fusion = (bf16[2048,1536]{1,0:T(8,128)(2,1)}, f32[2048,1536]{1,0:T(8,128)}) fusion(f32[1536]{0:T(1024)S(1)} %convert_element_type.166, bf16[2048,768]{1,0:T(8,128)(2,1)} %bitcast.151, bf16[768,1536]{1,0:T(8,128)(2,1)S(1)} %copy-done), kind=kOutput, calls=%fused_computation.20 | convolution fusion | flops 4863295488 | bytes 24385536 | tf_op jit(solution)/shard_map/dot_general | solution.py:96
  175.9 33.1 %all-gather.8.cloned.1.call-done = bf16[4,512,768]{2,1,0:T(8,128)(2,1)} async-done(((bf16[4,256,768]{2,1,0:T(8,128)(2,1)}), bf16[4,512,768]{2,1,0:T(8,128)(2,1)}) %all-gather.8.cloned.1.call-update) | async-done | bytes 3145744 | tf_op jit(solution)/shard_map/all_gather | solution.py:108
  209.0 16.6 %fusion.90 = (bf16[1536]{0:T(1024)(128)(2,1)S(1)}, bf16[2048,1536]{1,0:T(8,128)(2,1)S(1)}) fusion(f32[2048,1536]{1,0:T(8,128)} %get-tuple-element.72, f32[1536]{0:T(1024)S(1)} %convert_element_type.166, bf16[2048,768]{1,0:T(8,128)(2,1)} %bitcast.153, bf16[1536,768]{1,0:T(8,128)(2,1)} %param.29), kind=kOutput, calls=%fused_computation.116 | convolution fusion | flops 4901042688 | bytes 24388608 | tf_op jit(solution)/shard_map/dot_general | solution.py:18
  225.7 6.5 convolution_convert_fusion.2
  233.8 9.7 %convolution_convert_fusion.3 = bf16[2048,768]{1,0:T(8,128)(2,1)} fusion(bf16[2048,1536]{1,0:T(8,128)(2,1)} %get-tuple-element.71, bf16[1536,768]{1,0:T(8,128)(2,1)S(1)} %copy-done.27), kind=kOutput, calls=%fused_computation.31 | convolution fusion | flops 4833411072 | bytes 11796480 | tf_op jit(solution)/shard_map/dot_general | solution.py:101
  244.2 31.5 %reduce-scatter.15.cloned.1.call-done = bf16[4,256,768]{2,1,0:T(8,128)(2,1)} async-done(((bf16[4,512,768]{2,1,0:T(8,128)(2,1)}), bf16[4,256,768]{2,1,0:T(8,128)(2,1)}) %reduce-scatter.15.cloned.1.call-update) | async-done | bytes 1572880 | tf_op jit(solution)/shard_map/reduce_scatter | solution.py:118
  275.7 2.2 convert_reduce_fusion
  277.9 3.5 fusion.30
  281.4 39.8 %reduce-scatter.13.cloned.1.call-done = bf16[4,256,768]{2,1,0:T(8,128)(2,1)} async-done(((bf16[4,512,768]{2,1,0:T(8,128)(2,1)}), bf16[4,256,768]{2,1,0:T(8,128)(2,1)}) %reduce-scatter.13.cloned.1.call-update) | async-done | bytes 1572880 | tf_op jit(solution)/shard_map/reduce_scatter | solution.py:104
  321.2 4.6 convert_reduce_fusion.2
  325.8 1.7 copy-done.7
  327.5 2.6 convolution_convert_fusion.4
  330.1 1.7 copy.53
  331.8 2.4 reshape.203
  334.2 28.2 %fusion.50 = bf16[4,12,64,512]{3,2,1,0:T(8,128)(2,1)} fusion(bf16[4,256,12,64]{1,0,3,2:T(4,128)(2,1)} %reshape.203, f32[4,12,256]{2,1,0:T(8,128)S(1)} %get-tuple-element.67, f32[12,256,512]{2,1,0:T(8,128)} %convert_element_type.157, pred[4,256,512]{2,1,0:T(8,128)(4,1)S(1)} %broadcast_compare_fusion), kind=kOutput, calls=%fused_computation.77 | convolution fusion | flops 838349312 | bytes 11583488 | tf_op jit(solution)/shard_map/shqk,sqhd->skhd/dot_general | solution.py:141
  362.5 4.6 copy.55
  368.3 9.8 %convolution_convert_fusion = bf16[1536,768]{0,1:T(8,128)(2,1)} fusion(bf16[2048,1536]{1,0:T(8,128)(2,1)} %get-tuple-element.71, bf16[2048,768]{1,0:T(8,128)(2,1)} %bitcast.154), kind=kOutput, calls=%fused_computation.28 | convolution fusion | flops 4833017856 | bytes 11796480 | tf_op jit(solution)/shard_map/dot_general | solution.py:12
  378.1 9.3 %convolution_convert_fusion.1 = bf16[768,1536]{1,0:T(8,128)(2,1)} fusion(bf16[2048,768]{1,0:T(8,128)(2,1)} %bitcast.152, bf16[2048,1536]{1,0:T(8,128)(2,1)} %copy-done.32), kind=kOutput, calls=%fused_computation.29 | convolution fusion | flops 4833017856 | bytes 11796480 | tf_op jit(solution)/shard_map/dot_general | solution.py:12
  387.5 21.6 %fusion = f32[4,12,256,512]{3,2,1,0:T(8,128)} fusion(bf16[4,512,12,64]{1,3,2,0:T(8,128)(2,1)} %bitcast.132, bf16[4,256,12,64]{1,0,3,2:T(4,128)(2,1)S(1)} %copy-done.9, f32[4,12,256,512]{3,2,1,0:T(8,128)} %get-tuple-element.68, f32[4,12,256]{2,1,0:T(8,128)S(1)} %get-tuple-element.67, f32[12,256,512]{2,1,0:T(8,128)} %convert_element_type.157, ...), kind=kOutput, calls=%fused_computation | convolution fusion | flops 830484992 | bytes 61915136 | tf_op jit(solution)/shard_map/sub | solution.py:139
  409.1 23.6 %multiply_reduce_fusion = bf16[12,256,512]{2,1,0:T(8,128)(2,1)} fusion(f32[4,12,256,512]{3,2,1,0:T(8,128)} %fusion, f32[4,12,256]{2,1,0:T(8,128)S(1)} %get-tuple-element.67, f32[4,12,256,512]{3,2,1,0:T(8,128)} %get-tuple-element.68, f32[12,256,512]{2,1,0:T(8,128)} %convert_element_type.157, pred[4,256,512]{2,1,0:T(8,128)(4,1)S(1)} %broadcast_compare_fusion, ...), kind=kOutput, calls=%fused_computation.6 | convolution fusion | flops 841482240 | bytes 65060864 | tf_op jit(solution)/shard_map/sqhd,skhd->shqk/dot_general | solution.py:136
  432.7 7.8 copy.58
  440.8 5.4 fusion.71
  446.4 4.6 convolution_bitcast_fusion
  451.1 1.8 convert_reduce_fusion.4
  452.9 17.9 %reduce-scatter.29.cloned.1.call-done = bf16[96,1]{1,0:T(8,128)(2,1)} async-done(((bf16[1536,1]{1,0:T(8,128)(2,1)}), bf16[96,1]{1,0:T(8,128)(2,1)}) %reduce-scatter.29.cloned.1.call-update) | async-done | bytes 208
  472.1 64.3 %reduce-scatter.27.cloned.1.call-done = bf16[1536,48]{0,1:T(8,128)(2,1)} async-done(((bf16[1536,768]{0,1:T(8,128)(2,1)}), bf16[1536,48]{0,1:T(8,128)(2,1)}) %reduce-scatter.27.cloned.1.call-update) | async-done | bytes 147472 | tf_op jit(solution)/shard_map/reduce_scatter | solution.py:179
  538.1 64.6 %reduce-scatter.25.cloned.1.call-done = bf16[48,1536]{1,0:T(8,128)(2,1)} async-done(((bf16[768,1536]{1,0:T(8,128)(2,1)}), bf16[48,1536]{1,0:T(8,128)(2,1)}) %reduce-scatter.25.cloned.1.call-update) | async-done | bytes 147472 | tf_op jit(solution)/shard_map/reduce_scatter | solution.py:173
  602.7 1.6 convert_element_type.191
  604.4 73.7 %reduce-scatter.21.cloned.1.call-done = bf16[12,256,32]{1,0,2:T(8,128)(2,1)} async-done(((bf16[12,256,512]{1,0,2:T(8,128)(2,1)}), bf16[12,256,32]{1,0,2:T(8,128)(2,1)}) %reduce-scatter.21.cloned.1.call-update) | async-done | bytes 196624 | tf_op jit(solution)/shard_map/reduce_scatter | solution.py:182
  678.1 1.8 copy.59
  679.9 1.7 convert_reduce_fusion.3
  681.6 4.9 fusion.48
  686.6 39.9 %all-reduce = f32[7,768]{1,0:T(8,128)S(1)} all-reduce(f32[7,768]{1,0:T(8,128)S(1)} %stack.31), channel_id=5, replica_groups=mesh['dp'=16,'mp'=2] {'dp','mp'}, use_global_device_ids=true, to_apply=%region_20.21.clone | all-reduce | flops 5376 | bytes 43008
  727.0 5.2 fusion.47
  732.2 50.8 %reduce-scatter.23.cloned.1.call-done = f32[24,768]{1,0:T(8,128)} async-done(((f32[768,768]{1,0:T(8,128)}), f32[24,768]{1,0:T(8,128)}) %reduce-scatter.23.cloned.1.call-update) | async-done | bytes 73744 | tf_op jit(solution)/shard_map/reduce_scatter | solution.py:169
  783.0 103.8 %reduce-scatter.19.cloned.1.call-done = f32[24,768]{1,0:T(8,128)} async-done(((f32[768,768]{1,0:T(8,128)}), f32[24,768]{1,0:T(8,128)}) %reduce-scatter.19.cloned.1.call-update) | async-done | bytes 73744 | tf_op jit(solution)/shard_map/reduce_scatter | solution.py:168
  (127 shorter events, 13.5 us)
Async XLA Ops:
  7.2 155.3 %copy-start = (bf16[768,1536]{1,0:T(8,128)(2,1)S(1)}, bf16[768,1536]{1,0:T(8,128)(2,1)}, u32[]{:S(2)}) copy-start(bf16[768,1536]{1,0:T(8,128)(2,1)} %param.27) | copy-start | bytes 7077892
  7.2 57.9 %all-gather.4.cloned.1.call-start = ((), (), s32[]{:S(2)}) async-start(), calls=%async_computation.9 | async-start | bytes 4718592 | tf_op jit(solution)/shard_map/all_gather | solution.py:72
  7.2 6.8 copy-start.3
  8.1 6.5 copy-start.10
  8.9 5.8 copy-start.19
  9.6 5.1 copy-start.30
  11.4 2.6 copy-start.17
  11.4 5.9 copy-start.12
  14.0 3.3 copy-start.14
  14.7 2.7 copy-start.23
  14.7 2.7 copy-start.24
  14.7 2.7 copy-start.25
  17.3 145.2 %all-gather.6.cloned.1.call-start = ((), (), s32[]{:S(2)}) async-start(), calls=%async_computation.10 | async-start | bytes 4718592 | tf_op jit(solution)/shard_map/all_gather | solution.py:93
  17.4 5.4 copy-start.16
  110.2 3.2 copy-start.4
  110.2 3.2 copy-start.28
  113.3 1.8 copy-start.8
  115.1 2.3 copy-start.2
  115.7 2.5 copy-start.21
  117.4 91.6 %all-gather.8.cloned.1.call-start = ((), (), s32[]{:S(2)}) async-start(), calls=%async_computation.12 | async-start | bytes 4718592 | tf_op jit(solution)/shard_map/all_gather | solution.py:108
  118.1 157.5 %reduce-scatter.15.cloned.1.call-start = ((), (), s32[]{:S(2)}) async-start(), calls=%async_computation.13 | async-start | bytes 4718592 | tf_op jit(solution)/shard_map/reduce_scatter | solution.py:118
  225.7 6.5 copy-start.32
  232.1 1.7 copy-start.27
  232.2 89.1 %reduce-scatter.13.cloned.1.call-start = ((), (), s32[]{:S(2)}) async-start(), calls=%async_computation.11 | async-start | bytes 4718592 | tf_op jit(solution)/shard_map/reduce_scatter | solution.py:104
  243.5 0.7 copy-start.26
  243.5 202.9 %reduce-scatter.17.cloned.1.call-start = ((), (), s32[]{:S(2)}) async-start(), calls=%async_computation.14 | async-start | bytes 4718592 | tf_op jit(solution)/shard_map/reduce_scatter | solution.py:145
  244.2 77.1 %copy-start.6 = (bf16[4,256,768]{2,1,0:T(8,128)(2,1)S(1)}, bf16[4,256,768]{2,1,0:T(8,128)(2,1)}, u32[]{:S(2)}) copy-start(bf16[4,256,768]{2,1,0:T(8,128)(2,1)} %param.31) | copy-start | bytes 4718596
  321.2 6.2 copy-start.29
  325.8 1.7 copy-start.7
  367.1 103.6 %reduce-scatter.29.cloned.1.call-start = ((), (), s32[]{:S(2)}) async-start(), calls=%async_computation.20 | async-start | bytes 417792
  368.2 168.2 %reduce-scatter.27.cloned.1.call-start = ((), (), s32[]{:S(2)}) async-start(), calls=%async_computation.19 | async-start | bytes 2506752 | tf_op jit(solution)/shard_map/reduce_scatter | solution.py:179
  378.1 9.5 %copy-start.9 = (bf16[4,256,12,64]{1,0,3,2:T(4,128)(2,1)S(1)}, bf16[4,256,12,64]{1,0,3,2:T(4,128)(2,1)}, u32[]{:S(2)}) copy-start(bf16[4,256,12,64]{1,0,3,2:T(4,128)(2,1)} %reshape.203) | copy-start | bytes 4718596
  378.1 224.6 %reduce-scatter.25.cloned.1.call-start = ((), (), s32[]{:S(2)}) async-start(), calls=%async_computation.18 | async-start | bytes 2506752 | tf_op jit(solution)/shard_map/reduce_scatter | solution.py:173
  387.5 290.6 %reduce-scatter.21.cloned.1.call-start = ((), (), s32[]{:S(2)}) async-start(), calls=%async_computation.16 | async-start | bytes 4456448 | tf_op jit(solution)/shard_map/reduce_scatter | solution.py:182
  440.5 5.9 copy-start.5
  440.5 5.9 copy-start.11
  440.5 5.9 copy-start.18
  440.6 5.9 copy-start.20
  440.6 5.9 copy-start.22
  440.6 342.4 %reduce-scatter.23.cloned.1.call-start = ((), (), s32[]{:S(2)}) async-start(), calls=%async_computation.17 | async-start | bytes 2433024 | tf_op jit(solution)/shard_map/reduce_scatter | solution.py:169
  446.3 440.5 %reduce-scatter.19.cloned.1.call-start = ((), (), s32[]{:S(2)}) async-start(), calls=%async_computation.15 | async-start | bytes 2433024 | tf_op jit(solution)/shard_map/reduce_scatter | solution.py:168
  451.0 230.5 %copy-start.13 = (f32[1,2,4,128]{3,1,2,0:T(2,128)S(1)}, f32[1,2,4,128]{3,1,2,0:T(2,128)}, u32[]{:S(2)}) copy-start(f32[1,2,4,128]{3,1,2,0:T(2,128)} %copy-done.12) | copy-start | bytes 12292
  451.0 230.5 %copy-start.15 = (f32[1,2,4,128]{3,1,2,0:T(2,128)S(1)}, f32[1,2,4,128]{3,1,2,0:T(2,128)}, u32[]{:S(2)}) copy-start(f32[1,2,4,128]{3,1,2,0:T(2,128)} %copy-done.14) | copy-start | bytes 12292
  451.0 230.5 %copy-start.31 = (bf16[768,768]{1,0:T(8,128)(2,1)S(1)}, bf16[768,768]{1,0:T(8,128)(2,1)}, u32[]{:S(2)}) copy-start(bf16[768,768]{1,0:T(8,128)(2,1)} %param.20) | copy-start | bytes 3538948
  727.0 159.8 %copy-start.1 = (bf16[768,1536]{1,0:T(8,128)(2,1)S(1)}, bf16[768,1536]{1,0:T(8,128)(2,1)}, u32[]{:S(2)}) copy-start(bf16[768,1536]{1,0:T(8,128)(2,1)} %param.27) | copy-start | bytes 7077892
Sparse Core Ops, SparseCore 0:
  17.4 47.6 all-gather.3
  117.5 44.9 all-gather.5
  164.0 44.9 all-gather.7
  232.3 43.3 reduce-scatter.14
  277.8 43.3 reduce-scatter.12
  367.3 43.3 reduce-scatter.16
  415.1 55.5 reduce-scatter.28
  474.5 61.8 reduce-scatter.26
  540.7 61.9 reduce-scatter.24
  606.4 71.6 reduce-scatter.20
  684.8 98.1 reduce-scatter.22
  788.7 98.0 reduce-scatter.18
where the time goes:
time: 895 us; the launch traced here: 894 us
  waiting for transfers between devices  548 us (61%)
  matrix products  201 us (22%)
  other arithmetic  56.8 us (6%)
  blocking collectives  39.9 us (4%)
  local copies, waits for them, and re-layouts  32.8 us (4%)
  between operations  14.9 us (2%)
    reduce_scatter x1, waiting for transfers between devices, shards(): lax.psum_scatter(grad_value_w, ('dp', 'mp'), scatter_dimension=0, tiled=T...  104 us
    reduce_scatter x1, waiting for transfers between devices, shards(): lax.psum_scatter(grad_logits.astype(jnp.bfloat16), 'dp', scatter_dimensio...  73.7 us
    reduce_scatter x1, waiting for transfers between devices, shards(): lax.psum_scatter(grad_up.astype(jnp.bfloat16), 'dp', scatter_dimension=0,...  64.6 us
    reduce_scatter x1, waiting for transfers between devices, shards(): lax.psum_scatter(grad_down.astype(jnp.bfloat16), 'dp', scatter_dimension=...  64.3 us
    reduce_scatter x1, waiting for transfers between devices, shards(): lax.psum_scatter(grad_out_w, ('dp', 'mp'), scatter_dimension=0, tiled=True)  50.8 us
    all_gather x1, waiting for transfers between devices, shards(): lax.all_gather(h2_low.reshape(seqs, local_len, width), 'mp', axis=1, tile...  44.3 us
    dot_general x1, matrix products, shards(): jnp.einsum('shqk,skhd->sqhd', probs_low, every_head, preferred_element_ty...  40.2 us
    unnamed x1, blocking collectives  39.9 us
  transfers between devices with their start and end apart: 12, of which 11 were waited for; matrix products, arithmetic and copies ran while one was open for 18% of the time, Pallas kernels for 0%

commit v1 on v0

--- a/solution.py
+++ b/solution.py
@@ -1,7 +1,665 @@
+import functools
+
 import jax
 import jax.numpy as jnp
 from jax import lax
+from jax.experimental import pallas as pl
+from jax.experimental.pallas import tpu as pltpu
 from jax.sharding import PartitionSpec as P
+
+F32 = jnp.float32
+BF16 = jnp.bfloat16
+GELU_A = 0.7978845608028654
+GELU_B = GELU_A * 0.044715
+MIB = 2**20
+
+
+def mm(left, right, left_dim, right_dim):
+    return lax.dot_general(
+        left, right, (((left_dim,), (right_dim,)), ((), ())), preferred_element_type=F32
+    )
+
+
+def unit_rows(x):
+    centred = x - jnp.mean(x, -1, keepdims=True)
+    scale = lax.rsqrt(jnp.mean(centred * centred, -1, keepdims=True) + 1e-05)
+    return centred * scale, scale
+
+
+def norm_back(grad, unit, scale, gain):
+    e = grad * gain
+    return scale * (
+        e - jnp.mean(e, -1, keepdims=True) - unit * jnp.mean(e * unit, -1, keepdims=True)
+    )
+
+
+def same_segment(offs, seg_col, seg_row, length):
+    own = seg_col[0, pl.ds(pl.multiple_of(offs[0], length), length), :]
+    return own == seg_row[0]
+
+
+def whole(shape):
+    return pl.BlockSpec(shape, lambda i, *_: (0,) * len(shape))
+
+
+def by_row(first, shape):
+    return pl.BlockSpec((1,) + shape, lambda i, *_: (first + i,) + (0,) * len(shape))
+
+
+def mix_kernel(chained, offs, x_own, x_other, seg_col, seg_row, expo, wv, bv, wo, bo, g1, b1, g2, b2, *rest):
+    h1, values, recip, mixed, resid, h2, h2t, ones = rest[7 if chained else 0 :]
+    length = x_own.shape[1]
+    heads = expo.shape[0]
+    ones[:, 128:] = jnp.ones_like(ones[:, 128:])
+    x = x_own[0].astype(F32)
+    for block, off in ((x, offs[0]), (x_other[0].astype(F32), offs[1])):
+        unit, _ = unit_rows(block)
+        at = pl.ds(pl.multiple_of(off, length), length)
+        h1[0, at, :] = (unit * g1[...] + b1[...]).astype(BF16)
+    values[0] = (mm(h1[0], wv[...], 1, 0) + bv[...]).astype(BF16)
+    mask = jnp.where(same_segment(offs, seg_col, seg_row, length), 1.0, 0.0).astype(BF16)
+    low_lane = lax.broadcasted_iota(jnp.int32, (length, 128), 1) < 64
+    for pair in range(heads // 2):
+        lanes = slice(128 * pair, 128 * pair + 128)
+        ones[:, :128] = values[0, :, lanes]
+        first = mm(expo[2 * pair] * mask, ones[...], 1, 0)
+        second = mm(expo[2 * pair + 1] * mask, ones[...], 1, 0)
+        inverse = 1.0 / jnp.where(low_lane, first[:, 128:], second[:, 128:])
+        recip[0, :, lanes] = inverse
+        mixed[0, :, lanes] = jnp.where(low_lane, first[:, :128], second[:, :128]) * inverse
+    r = x + mm(mixed[0].astype(BF16), wo[...], 1, 0) + bo[...]
+    resid[0] = r
+    unit, _ = unit_rows(r)
+    low = (unit * g2[...] + b2[...]).astype(BF16)
+    h2[0] = low
+    h2t[...] = low.T
+
+
+def mix_rows(first, count, offs, inputs, received, seg_col, seg_row, expo, weights, chain):
+    rows, length, width = inputs.shape
+    full = seg_row.shape[2]
+    heads = expo.shape[0]
+    shapes = [
+        ((full, width), BF16),
+        ((full, width), BF16),
+        ((length, width), F32),
+        ((length, width), F32),
+        ((length, width), F32),
+        ((length, width), BF16),
+    ]
+    out_specs = [by_row(first, s) for s, _ in shapes]
+    out_specs.append(pl.BlockSpec((width, length), lambda i, *_: (0, first + i)))
+    out_shape = [jax.ShapeDtypeStruct((rows,) + s, t) for s, t in shapes]
+    out_shape.append(jax.ShapeDtypeStruct((width, rows * length), BF16))
+    operands = [offs, inputs, received, seg_col, seg_row, expo, *weights]
+    in_specs = [
+        by_row(first, (length, width)),
+        by_row(0, (length, width)),
+        by_row(first, (full, 1)),
+        by_row(first, (1, full)),
+        whole(expo.shape),
+        *[whole(w.shape) for w in weights],
+    ]
+    aliases = {}
+    if chain is not None:
+        aliases = {len(operands) + i: i for i in range(len(out_shape))}
+        operands += list(chain)
+        in_specs += [pl.BlockSpec(memory_space=pl.ANY)] * len(out_shape)
+    flops = 2 * count * (2 * full * width * width // 2 * 2 + length * width * width + heads * length * full * 256)
+    return pl.pallas_call(
+        functools.partial(mix_kernel, chain is not None),
+        grid_spec=pltpu.PrefetchScalarGridSpec(
+            num_scalar_prefetch=1,
+            grid=(count,),
+            in_specs=in_specs,
+            out_specs=out_specs,
+            scratch_shapes=[pltpu.VMEM((full, 256), BF16)],
+        ),
+        out_shape=out_shape,
+        input_output_aliases=aliases,
+        compiler_params=pltpu.CompilerParams(vmem_limit_bytes=40 * MIB),
+        cost_estimate=pl.CostEstimate(flops=flops, bytes_accessed=10 * MIB, transcendentals=0),
+        name="mix_rows",
+    )(*operands)
+
+
+def gelu_pair(t):
+    square = t * t
+    curve = jnp.tanh(t * (GELU_A + GELU_B * square))
+    half = 0.5 + 0.5 * curve
+    act = t * half
+    return act, half + act * (1.0 - curve) * (GELU_A + 3 * GELU_B * square)
+
+
+def hidden_tile(h2, g, h2t, gt, wu, bu, wd, out, dh, grads, bias, act_s, pre_s, block):
+    total = jnp.zeros(bias.shape, F32)
+    for m in range(h2.shape[0] // block):
+        at = pl.ds(m * block, block)
+        pre = mm(h2[at, :], wu, 1, 0) + bu
+        grad_act = mm(g[at, :], wd, 1, 1)
+        act, slope = gelu_pair(pre)
+        act_low = act.astype(BF16)
+        grad_pre = grad_act * slope
+        total += jnp.sum(grad_pre, 0, keepdims=True)
+        pre_low = grad_pre.astype(BF16)
+        act_s[at, :] = act_low
+        pre_s[at, :] = pre_low
+        out[at, :] += mm(act_low, wd, 1, 0)
+        dh[at, :] += mm(pre_low, wu, 1, 1)
+    bias[...] = total
+    grads[0] = mm(h2t[...], pre_s[...], 1, 0).astype(BF16)
+    grads[1] = mm(gt[...], act_s[...], 1, 0).astype(BF16)
+
+
+def own_hidden_kernel(block, core, h2, g, h2t, gt, wu, bu, wd, out, dh, theirs, mine, b_theirs, b_mine, act_s, pre_s):
+    step = pl.program_id(0)
+
+    @pl.when(step == 0)
+    def _():
+        out[...] = jnp.zeros_like(out)
+        dh[...] = jnp.zeros_like(dh)
+
+    for at, grads, bias in ((0, theirs, b_theirs), (1, mine, b_mine)):
+
+        @pl.when(step == at)
+        def _(grads=grads, bias=bias):
+            hidden_tile(h2, g, h2t, gt, wu[...], bu[...], wd[...], out, dh, grads, bias, act_s, pre_s, block)
+
+
+def packed_tile(w, width):
+    return w[:width, :], w[2 * width :, :][:1].astype(F32), w[width : 2 * width, :]
+
+
+def other_hidden_kernel(block, h2, g, h2t, gt, w_mine, w_theirs, out0, dh0, out, dh, mine, theirs, b_mine, b_theirs, act_s, pre_s):
+    step = pl.program_id(0)
+    width = h2.shape[1]
+
+    @pl.when(step == 0)
+    def _():
+        out[...] = out0[...]
+        dh[...] = dh0[...]
+
+    for at, w, grads, bias in ((0, w_mine, mine, b_mine), (1, w_theirs, theirs, b_theirs)):
+
+        @pl.when(step == at)
+        def _(w=w, grads=grads, bias=bias):
+            hidden_tile(h2, g, h2t, gt, *packed_tile(w, width), out, dh, grads, bias, act_s, pre_s, block)
+
+
+def hidden_params(positions, width, tile, steps):
+    return dict(
+        scratch_shapes=[pltpu.VMEM((positions, tile), BF16), pltpu.VMEM((positions, tile), BF16)],
+    ), dict(
+        compiler_params=pltpu.CompilerParams(vmem_limit_bytes=56 * MIB),
+        cost_estimate=pl.CostEstimate(
+            flops=12 * positions * width * tile * steps,
+            bytes_accessed=24 * MIB,
+            transcendentals=positions * tile * steps,
+        ),
+    )
+
+
+def own_hidden(core, h2, g, h2t, gt, wu, bu, wd):
+    positions, width = h2.shape
+    tile = wu.shape[1] // 2
+    scratch, call = hidden_params(positions, width, tile, 2)
+    pick = lambda i, core: lax.rem(i + 1 + core[0], 2)
+    return pl.pallas_call(
+        functools.partial(own_hidden_kernel, 256),
+        grid_spec=pltpu.PrefetchScalarGridSpec(
+            num_scalar_prefetch=1,
+            grid=(2,),
+            in_specs=[
+                whole(h2.shape),
+                whole(g.shape),
+                whole(h2t.shape),
+                whole(gt.shape),
+                pl.BlockSpec((width, tile), lambda i, core: (0, pick(i, core))),
+                pl.BlockSpec((1, tile), lambda i, core: (0, pick(i, core))),
+                pl.BlockSpec((tile, width), lambda i, core: (pick(i, core), 0)),
+            ],
+            out_specs=[whole((positions, width))] * 2 + [whole((2, width, tile))] * 2 + [whole((1, tile))] * 2,
+            **scratch,
+        ),
+        out_shape=[jax.ShapeDtypeStruct((positions, width), F32)] * 2
+        + [jax.ShapeDtypeStruct((2, width, tile), BF16)] * 2
+        + [jax.ShapeDtypeStruct((1, tile), F32)] * 2,
+        name="own_hidden",
+        **call,
+    )(core, h2, g, h2t, gt, wu, bu, wd)
+
+
+def other_hidden(h2, g, h2t, gt, w_mine, w_theirs, out0, dh0):
+    positions, width = h2.shape
+    tile = w_mine.shape[1]
+    scratch, call = hidden_params(positions, width, tile, 2)
+    operands = (h2, g, h2t, gt, w_mine, w_theirs, out0, dh0)
+    return pl.pallas_call(
+        functools.partial(other_hidden_kernel, 256),
+        grid=(2,),
+        in_specs=[whole(a.shape) for a in operands],
+        out_specs=[whole((positions, width))] * 2 + [whole((2, width, tile))] * 2 + [whole((1, tile))] * 2,
+        out_shape=[jax.ShapeDtypeStruct((positions, width), F32)] * 2
+        + [jax.ShapeDtypeStruct((2, width, tile), BF16)] * 2
+        + [jax.ShapeDtypeStruct((1, tile), F32)] * 2,
+        name="other_hidden",
+        **scratch,
+        **call,
+    )(*operands)
+
+
+def back_kernel(chained, offs, out_acc, dh, resid, g, mixed, recip, x_own, x_other, seg_col, seg_row, expo, wo, wv, g2, bd, *rest):
+    layer_out, grad_resid, gm, gv, gh_own, gh_send, vec_two, vec_one, gmt, gvt, gh = rest[8 if chained else 0 :]
+    length = x_own.shape[1]
+    heads = expo.shape[0]
+    r = resid[0]
+    layer_out[0] = (r + out_acc[0] + bd[...]).astype(BF16)
+    unit, scale = unit_rows(r)
+    grad = dh[0]
+    cot = g[0].astype(F32)
+    total = cot + norm_back(grad, unit, scale, g2[...])
+    grad_resid[0] = total
+    grad_o = total.astype(BF16)
+    vec_two[0, 0:1, :] = jnp.sum(grad_o.astype(F32), 0, keepdims=True)
+    vec_two[0, 1:2, :] = jnp.sum(grad * unit, 0, keepdims=True)
+    vec_two[0, 2:3, :] = jnp.sum(grad, 0, keepdims=True)
+    vec_two[0, 3:4, :] = jnp.sum(cot, 0, keepdims=True)
+    scaled = (mm(grad_o, wo[...], 1, 1).astype(BF16).astype(F32) * recip[0]).astype(BF16)
+    gm[0] = scaled
+    gmt[...] = scaled.T
+    mask = jnp.where(same_segment(offs, seg_col, seg_row, length), 1.0, 0.0).astype(BF16)
+    for head in range(heads):
+        at = slice(64 * head, 64 * head + 64)
+        gvt[at, :] = mm(gmt[at, :], expo[head] * mask, 1, 0).astype(BF16)
+    values_grad = gvt[...].T
+    gv[0] = values_grad
+    gh[...] = mm(values_grad, wv[...], 1, 1)
+    gain = jnp.zeros((1, gh.shape[1]), F32)
+    for block, off in ((x_own, offs[0]), (x_other, offs[1])):
+        unit, _ = unit_rows(block[0].astype(F32))
+        gain += jnp.sum(gh[pl.ds(pl.multiple_of(off, length), length), :] * unit, 0, keepdims=True)
+    vec_one[0, 0:1, :] = gain
+    vec_one[0, 1:2, :] = jnp.sum(gh[...], 0, keepdims=True)
+    vec_one[0, 2:3, :] = jnp.sum(values_grad.astype(F32), 0, keepdims=True)
+    gh_own[0] = gh[pl.ds(pl.multiple_of(offs[0], length), length), :]
+    gh_send[0] = gh[pl.ds(pl.multiple_of(offs[1], length), length), :].astype(BF16)
+
+
+def back_rows(first, count, offs, row_arrays, received, seg_col, seg_row, expo, weights, chain):
+    rows, length, width = row_arrays[0].shape
+    full = seg_row.shape[2]
+    shapes = [
+        ((length, width), BF16),
+        ((length, width), F32),
+        ((length, width), BF16),
+        ((full, width), BF16),
+        ((length, width), F32),
+        ((4, width), F32),
+        ((3, width), F32),
+    ]
+    out_specs = [by_row(first, s) for s, _ in shapes]
+    out_shape = [jax.ShapeDtypeStruct((rows,) + s, t) for s, t in shapes]
+    out_specs.insert(5, by_row(0, (length, width)))
+    out_shape.insert(5, jax.ShapeDtypeStruct((count, length, width), BF16))
+    operands = [offs, *row_arrays, received, seg_col, seg_row, expo, *weights]
+    in_specs = [by_row(first, (length, width)) for _ in row_arrays]
+    in_specs += [
+        by_row(0, (length, width)),
+        by_row(first, (full, 1)),
+        by_row(first, (1, full)),
+        whole(expo.shape),
+        *[whole(w.shape) for w in weights],
+    ]
+    aliases = {}
+    if chain is not None:
+        keep = [i for i in range(len(out_shape))]
+        aliases = {len(operands) + i: i for i in keep if i != 5}
+        operands += list(chain)
+        in_specs += [pl.BlockSpec(memory_space=pl.ANY)] * len(out_shape)
+    return pl.pallas_call(
+        functools.partial(back_kernel, chain is not None),
+        grid_spec=pltpu.PrefetchScalarGridSpec(
+            num_scalar_prefetch=1,
+            grid=(count,),
+            in_specs=in_specs,
+            out_specs=out_specs,
+            scratch_shapes=[
+                pltpu.VMEM((width, length), BF16),
+                pltpu.VMEM((width, full), BF16),
+                pltpu.VMEM((full, width), F32),
+            ],
+        ),
+        out_shape=out_shape,
+        input_output_aliases=aliases,
+        compiler_params=pltpu.CompilerParams(vmem_limit_bytes=48 * MIB),
+        cost_estimate=pl.CostEstimate(flops=4 * 10**9 * count, bytes_accessed=14 * MIB, transcendentals=0),
+        name="back_rows",
+    )(*operands)
+
+
+def logits_kernel(offs, gm, mixed, values, seg_col, seg_row, expo, theirs, mine, ones, masks):
+    step = pl.program_id(0)
+    rows, length = gm.shape[:2]
+    half = pl.num_programs(0) // 2
+
+    @pl.when(step == 0)
+    def _():
+        ones[:, 128:] = jnp.ones_like(ones[:, 128:])
+        own = pl.ds(pl.multiple_of(offs[0], length), length)
+        for row in range(rows):
+            masks[row] = jnp.where(seg_col[row, own, :] == seg_row[row], 1.0, 0.0)
+
+    low_lane = lax.broadcasted_iota(jnp.int32, (length, 128), 1) < 64
+    zero = jnp.zeros((length, 128), F32)
+    sums = [None, None]
+    for row in range(rows):
+        ones[:, :128] = values[row]
+        scaled = gm[row].astype(F32)
+        product = scaled * mixed[row]
+        high = product.astype(BF16).astype(F32)
+        rest = product - high
+        turned_high = pltpu.roll(high, 64, 1)
+        turned_rest = pltpu.roll(rest, 64, 1)
+        for head in range(2):
+            keep = low_lane if head == 0 else jnp.logical_not(low_lane)
+            left = jnp.concatenate(
+                [
+                    jnp.where(keep, scaled, zero).astype(BF16),
+                    (-jnp.where(keep, high, turned_rest)).astype(BF16),
+                ],
+                axis=1,
+            )
+            part = mm(left, ones[...], 1, 1) * masks[row]
+            sums[head] = part if sums[head] is None else sums[head] + part
+    for head in range(2):
+        grad = (expo[head].astype(F32) * sums[head]).astype(BF16).T
+
+        @pl.when(step < half)
+        def _(head=head, grad=grad):
+            theirs[head] = grad
+
+        @pl.when(step >= half)
+        def _(head=head, grad=grad):
+            mine[head] = grad
+
+
+def logits_grad(offs, gm, mixed, values, seg_col, seg_row, expo):
+    rows, length, width = gm.shape
+    heads, _, full = expo.shape
+    pairs = heads // 2
+    half = pairs // 2
+    pick = lambda i, offs: lax.rem(i + half * (1 + offs[2]), pairs)
+    return pl.pallas_call(
+        logits_kernel,
+        grid_spec=pltpu.PrefetchScalarGridSpec(
+            num_scalar_prefetch=1,
+            grid=(pairs,),
+            in_specs=[
+                pl.BlockSpec((rows, length, 128), lambda i, offs: (0, 0, pick(i, offs))),
+                pl.BlockSpec((rows, length, 128), lambda i, offs: (0, 0, pick(i, offs))),
+                pl.BlockSpec((rows, full, 128), lambda i, offs: (0, 0, pick(i, offs))),
+                whole(seg_col.shape),
+                whole(seg_row.shape),
+                pl.BlockSpec((2, length, full), lambda i, offs: (pick(i, offs), 0, 0)),
+            ],
+            out_specs=[
+                pl.BlockSpec((2, full, length), lambda i, offs: (jnp.minimum(i, half - 1), 0, 0)),
+                pl.BlockSpec((2, full, length), lambda i, offs: (jnp.maximum(i - half, 0), 0, 0)),
+            ],
+            scratch_shapes=[pltpu.VMEM((full, 256), BF16), pltpu.VMEM((rows, length, full), F32)],
+        ),
+        out_shape=[jax.ShapeDtypeStruct((heads // 2, full, length), BF16)] * 2,
+        compiler_params=pltpu.CompilerParams(vmem_limit_bytes=40 * MIB),
+        cost_estimate=pl.CostEstimate(
+            flops=2 * rows * heads * length * full * 256, bytes_accessed=16 * MIB, transcendentals=0
+        ),
+        name="logits_grad",
+    )(offs, gm, mixed, values, seg_col, seg_row, expo)
+
+
+def square_kernel(core, mixed, grad_resid, h1, gv, vectors, theirs, mine):
+    width = mixed.shape[1]
+    out_w = mm(mixed[...].astype(BF16), grad_resid[...].astype(BF16), 0, 0).astype(BF16)
+    value_w = mm(h1[...], gv[...], 0, 0).astype(BF16)
+    for at, (first, second) in enumerate(((mine, theirs), (theirs, mine))):
+
+        @pl.when(core[0] == at)
+        def _(first=first, second=second):
+            first[:, :width] = out_w
+            second[:, :width] = value_w
+            first[:, width:] = vectors[...]
+            second[:, width:] = jnp.zeros_like(vectors)
+
+
+def square_grads(core, mixed, grad_resid, h1, gv, vectors):
+    width = mixed.shape[1]
+    operands = (mixed, grad_resid, h1, gv, vectors)
+    shape = (width, width + 128)
+    return pl.pallas_call(
+        square_kernel,
+        grid_spec=pltpu.PrefetchScalarGridSpec(
+            num_scalar_prefetch=1,
+            grid=(1,),
+            in_specs=[whole(a.shape) for a in operands],
+            out_specs=[whole(shape)] * 2,
+        ),
+        out_shape=[jax.ShapeDtypeStruct(shape, BF16)] * 2,
+        compiler_params=pltpu.CompilerParams(vmem_limit_bytes=48 * MIB),
+        cost_estimate=pl.CostEstimate(
+            flops=2 * width * width * (mixed.shape[0] + h1.shape[0]), bytes_accessed=16 * MIB, transcendentals=0
+        ),
+        name="square_grads",
+    )(core, *operands)
+
+
+def input_kernel(chained, x, grad_resid, gh_own, gh_received, g1, *rest):
+    grad = rest[1 if chained else 0]
+    unit, scale = unit_rows(x[0].astype(F32))
+    total = gh_own[0] + gh_received[0].astype(F32)
+    grad[0] = grad_resid[0] + norm_back(total, unit, scale, g1[...])
+
+
+def input_rows(first, count, inputs, grad_resid, gh_own, gh_received, g1, chain):
+    rows, length, width = inputs.shape
+    operands = [inputs, grad_resid, gh_own, gh_received, g1]
+    in_specs = [by_row(first, (length, width))] * 3 + [by_row(0, (length, width)), whole(g1.shape)]
+    aliases = {}
+    if chain is not None:
+        aliases = {len(operands): 0}
+        operands.append(chain)
+        in_specs.append(pl.BlockSpec(memory_space=pl.ANY))
+    return pl.pallas_call(
+        functools.partial(input_kernel, chain is not None),
+        grid=(count,),
+        in_specs=in_specs,
+        out_specs=by_row(first, (length, width)),
+        out_shape=jax.ShapeDtypeStruct((rows, length, width), F32),
+        input_output_aliases=aliases,
+        compiler_params=pltpu.CompilerParams(vmem_limit_bytes=24 * MIB),
+        cost_estimate=pl.CostEstimate(flops=10**7, bytes_accessed=4 * MIB, transcendentals=0),
+        name="input_rows",
+    )(*operands)
+
+
+def swap(a, axis, size, bit):
+    return lax.ppermute(a, axis, [(i, i ^ bit) for i in range(size)])
+
+
+def total(parts):
+    out = parts[0].astype(F32)
+    for p in parts[1:]:
+        out = out + p.astype(F32)
+    return out
+
+
+def halve(parts, dim, bit, axis, size, step):
+    pick = lambda p, b: lax.dynamic_index_in_dim(p, b, dim, keepdims=False)
+    sent = total([pick(p, 1 - bit) for p in parts]).astype(BF16)
+    return [pick(p, bit) for p in parts] + [swap(sent, axis, size, step)]
+
+
+def paired_shards(
+    dp,
+    mp,
+    inputs,
+    segment_ids,
+    ln1_gain,
+    ln1_bias,
+    value_weight,
+    value_bias,
+    random_logits,
+    out_weight,
+    out_bias,
+    ln2_gain,
+    ln2_bias,
+    up_weight,
+    up_bias,
+    down_weight,
+    down_bias,
+    out_cotangent,
+):
+    rows, length, width = inputs.shape
+    heads = random_logits.shape[0]
+    full = segment_ids.shape[1]
+    positions = rows * length
+    hidden = up_weight.shape[1]
+    tile = hidden // 2
+    me = lax.axis_index("mp")
+    place = lax.axis_index("dp")
+    bits = dp.bit_length() - 1
+    bit = [lax.rem(lax.div(place, 1 << b), 2) for b in range(bits)]
+    core = bit[0]
+    core_at = core.reshape(1).astype(jnp.int32)
+    offs = jnp.stack([me * length, (1 - me) * length, core]).astype(jnp.int32)
+    row_vector = lambda v: v.astype(F32).reshape(1, -1)
+    g1, b1, g2, b2 = (row_vector(v) for v in (ln1_gain, ln1_bias, ln2_gain, ln2_bias))
+    bv, bo, bd = (row_vector(v) for v in (value_bias, out_bias, down_bias))
+
+    received = [swap(inputs[r : r + 1], "mp", mp, 1) for r in range(rows)]
+    column = core * tile
+    packed = jnp.concatenate(
+        [
+            lax.dynamic_slice_in_dim(up_weight, column, tile, 1),
+            lax.dynamic_slice_in_dim(down_weight, column, tile, 0),
+            jnp.broadcast_to(lax.dynamic_slice_in_dim(up_bias, column, tile, 0)[None], (16, tile)),
+        ],
+        axis=0,
+    )
+    packed, _ = lax.optimization_barrier((packed, received[1]))
+    w_mine = swap(packed, "mp", mp, 1)
+    w_theirs = swap(w_mine, "dp", dp, 1)
+
+    expo = jnp.exp(random_logits.astype(F32)).astype(BF16)
+    seg_col = segment_ids[:, :, None]
+    seg_row = segment_ids[:, None, :]
+    g = out_cotangent.reshape(positions, width)
+    gt = g.T
+
+    chain = None
+    for r in range(rows):
+        chain = mix_rows(
+            r,
+            1,
+            offs,
+            inputs,
+            received[r],
+            seg_col,
+            seg_row,
+            expo,
+            (value_weight, bv, out_weight, bo, g1, b1, g2, b2),
+            chain,
+        )
+    h1, values, recip, mixed, resid, h2, h2t = chain
+    h2 = h2.reshape(positions, width)
+    out, dh, own_theirs, own_mine, b_own_theirs, b_own_mine = own_hidden(
+        core_at, h2, g, h2t, gt, up_weight, row_vector(up_bias), down_weight
+    )
+    out, dh, other_mine, other_theirs, b_other_mine, b_other_theirs = other_hidden(
+        h2, g, h2t, gt, w_mine, w_theirs, out, dh
+    )
+
+    shape = (rows, length, width)
+    row_arrays = [out.reshape(shape), dh.reshape(shape), resid, out_cotangent, mixed, recip, inputs]
+    chain = None
+    passed = []
+    for r in range(rows):
+        chain = back_rows(
+            r, 1, offs, row_arrays, received[r], seg_col, seg_row, expo, (out_weight, value_weight, g2, bd), chain
+        )
+        passed.append(swap(chain[5], "mp", mp, 1))
+    layer_out, grad_resid, gm, gv, gh_own, _, vec_two, vec_one = chain
+
+    logits_theirs, logits_mine = logits_grad(offs, gm, mixed, values, seg_col, seg_row, expo)
+
+    by_core = lambda first, second: jnp.where(core == 0, first, second)
+    in_order = lambda mine, theirs, dim: by_core(
+        jnp.concatenate([mine, theirs], dim), jnp.concatenate([theirs, mine], dim)
+    )
+    bias_own = in_order(b_own_mine, b_own_theirs, 1)
+    bias_other = in_order(b_other_mine, b_other_theirs, 1)
+    bias_all = jnp.where(
+        me == 0, jnp.concatenate([bias_own, bias_other], 0), jnp.concatenate([bias_other, bias_own], 0)
+    )
+    bias_columns = bias_all.reshape(mp, dp, hidden // dp).transpose(1, 0, 2).reshape(width, -1)
+    vectors = jnp.concatenate([jnp.sum(vec_two, 0), jnp.sum(vec_one, 0)], 0).T
+    used = vectors.shape[1]
+    vectors = jnp.concatenate([vectors, bias_columns], 1).astype(BF16)
+    vectors = jnp.pad(vectors, ((0, 0), (0, 128 - vectors.shape[1])))
+    square_theirs, square_mine = square_grads(
+        core_at,
+        mixed.reshape(positions, width),
+        grad_resid.reshape(positions, width),
+        h1.reshape(rows * full, width),
+        gv.reshape(rows * full, width),
+        vectors,
+    )
+
+    def scatter(mine, theirs, lead, rest):
+        parts = [mine, swap(theirs, "dp", dp, 1)]
+        parts = [p.reshape(lead + (2,) * (bits - 1) + rest) for p in parts]
+        for b in range(1, bits):
+            parts = halve(parts, len(lead) + bits - 1 - b, bit[b], "dp", dp, 1 << b)
+        return parts
+
+    def over_cores(parts, dim):
+        whole_sum = total(parts)
+        pick = lambda b: lax.dynamic_index_in_dim(whole_sum, b, dim, keepdims=False)
+        return pick(core), swap(pick(1 - core).astype(BF16), "dp", dp, 1).astype(F32)
+
+    hidden_shape = (2, width // dp, tile)
+    own = scatter(own_mine, own_theirs, (2,), hidden_shape)
+    other = scatter(other_mine, other_theirs, (2,), hidden_shape)
+    own.append(swap(total(other).astype(BF16), "mp", mp, 1))
+    weight_parts = in_order(*over_cores(own, 1), 2)
+    logit_parts = scatter(logits_mine, logits_theirs, (heads // 2,), (2, full // dp, length))
+    logit_part = in_order(*over_cores(logit_parts, 1), 0).transpose(0, 2, 1)
+    square = scatter(square_mine, square_theirs, (), (2, mp, width // (dp * mp), width + 128))
+    square = halve(square, 1, me, "mp", mp, 1)
+    kept, other_kept = over_cores(square, 0)
+    first, second = by_core(kept, other_kept), by_core(other_kept, kept)
+    vector_part = first[:, width:]
+    column = lambda i: vector_part[:, i]
+
+    chain = None
+    for r in range(rows):
+        chain = input_rows(r, 1, inputs, grad_resid, gh_own, passed[r], g1, chain)
+    return (
+        layer_out,
+        chain,
+        column(4),
+        column(5),
+        second[:, :width],
+        column(6),
+        logit_part,
+        first[:, :width],
+        column(0),
+        column(1),
+        column(2),
+        weight_parts[0],
+        vector_part[:, used : used + hidden // dp // (width // (dp * mp))].reshape(1, -1),
+        weight_parts[1].T,
+        column(3),
+    )
 
 
 def smooth(t):
@@ -238,4 +896,6 @@
         P("mp", "dp"),
         P(("dp", "mp")),
     )
-    return jax.shard_map(shards, mesh=mesh, in_specs=in_specs, out_specs=out_specs, check_vma=False)
+    dp, mp = mesh.shape["dp"], mesh.shape["mp"]
+    body = functools.partial(paired_shards, dp, mp) if mp == 2 else shards
+    return jax.shard_map(body, mesh=mesh, in_specs=in_specs, out_specs=out_specs, check_vma=False)

time: 895 us -> 369 us (0.41)
  waiting for transfers between devices: 548 us -> 120 us
  matrix products: 201 us -> 0 us
  Pallas kernels: 0 us -> 133 us
  blocking collectives: 39.9 us -> 0 us
  starting transfers between devices: 0.71 us -> 35 us
  other arithmetic: 56.8 us -> 39.9 us
  between operations: 14.9 us -> 1.52 us
    reduce_scatter x8 -> x0, waiting for transfers between devices: 429 us -> none  [the longest x1 104 us: shards(): lax.psum_scatter(grad_value_w, ('dp', 'mp'), scatter_dimension=0, tiled=T...]
    dot_general x15 -> x0, matrix products: 179 us -> none  [the longest x1 40.2 us: shards(): jnp.einsum('shqk,skhd->sqhd', probs_low, every_head, preferred_element_ty...]
    pallas_call x0 -> x16, Pallas kernels: none -> 133 us  [the longest x4 30.2 us: back_rows(): pl.pallas_call(functools.partial(back_kernel, chain is not None), grid_sp...]
    ppermute x0 -> x31, waiting for transfers between devices: none -> 120 us  [swap(): return lax.ppermute(a, axis, [(i, i ^ bit) for i in range(size)])]
    all_gather x3 -> x0, waiting for transfers between devices: 101 us -> none  [the longest x1 44.3 us: shards(): lax.all_gather(h2_low.reshape(seqs, local_len, width), 'mp', axis=1, tile...]
    unnamed x1 -> x0, blocking collectives: 39.9 us -> none
    ppermute x0 -> x31, starting transfers between devices: none -> 35 us  [swap(): return lax.ppermute(a, axis, [(i, i ^ bit) for i in range(size)])]
    sub x1 -> x0, matrix products: 21.6 us -> none  [shards(): grad_probs - jnp.sum(probs * grad_probs, -1, keepdims=True)]
  transfers between devices with their start and end apart: 12 -> 31, of which waited for: 11 -> 16; matrix products, arithmetic and copies ran while one was open for 18% -> 15% of each run, Pallas kernels for 0% -> 36%
where the time goes in v1:
time: 369 us; the launch traced here: 365 us
  Pallas kernels  133 us (36%)
  waiting for transfers between devices  120 us (33%)
  other arithmetic  39.9 us (11%)
  local copies, waits for them, and re-layouts  35.8 us (10%)
  starting transfers between devices  35 us (9%)
    ppermute x31, waiting for transfers between devices, swap(): return lax.ppermute(a, axis, [(i, i ^ bit) for i in range(size)])  120 us
    ppermute x31, starting transfers between devices, swap(): return lax.ppermute(a, axis, [(i, i ^ bit) for i in range(size)])  35 us
    pallas_call x4, Pallas kernels, back_rows(): pl.pallas_call(functools.partial(back_kernel, chain is not None), grid_sp...  30.2 us
    pallas_call x1, Pallas kernels, other_hidden(): pl.pallas_call(functools.partial(other_hidden_kernel, 256), grid=(2,), in...  26.6 us
    pallas_call x4, Pallas kernels, mix_rows(): pl.pallas_call(functools.partial(mix_kernel, chain is not None), grid_spe...  26.5 us
    pallas_call x1, Pallas kernels, own_hidden(): pl.pallas_call(functools.partial(own_hidden_kernel, 256), grid_spec=pltpu...  24.1 us
    convert_element_type x13, other arithmetic, halve(): sent = total([pick(p, 1 - bit) for p in parts]).astype(BF16)  22.4 us
    unnamed x110, local copies, waits for them, and re-layouts  16.1 us
  transfers between devices with their start and end apart: 31, of which 16 were waited for; matrix products, arithmetic and copies ran while one was open for 15% of the time, Pallas kernels for 36%

profile of v1, /device:TPU:0, one launch (start us, length us, event | category | flops | bytes accessed | tf_op | source)
XLA Modules:
  0.0 365.2 jit_solution(17005114052778371917)
XLA Ops:
  0.7 2.5 fusion.28
  3.2 2.9 collective-permute-start.2
  7.8 7.4 %collective-permute-done.2.x_other = bf16[1,256,768]{2,1,0:T(8,128)(2,1)S(1)} collective-permute-done((bf16[1,256,768]{2,1,0:T(8,128)(2,1)S(1)}, bf16[1,256,768]{2,1,0:T(8,128)(2,1)S(1)}, u32[]{:S(2)}, u32[]{:S(2)}) %collective-permute-start.2) | collective-permute-done | bytes 393248 | tf_op jit(solution)/shard_map/ppermute | solution.py:485
  15.3 1.7 collective-permute-start.4
  17.3 1.7 collective-permute-start.1
  19.4 4.5 %exponential_convert_fusion.expo = bf16[12,256,512]{2,1,0:T(8,128)(2,1)} fusion(bf16[12,256,512]{2,1,0:T(8,128)(2,1)} %param.22), kind=kLoop, calls=%fused_computation | loop fusion | flops 3145728 | bytes 6291456 | tf_op jit(solution)/shard_map/convert_element_type | solution.py:552
  23.9 46.2 %collective-permute-done.4.w_mine = bf16[1552,768]{1,0:T(8,128)(2,1)} collective-permute-done((bf16[1552,768]{1,0:T(8,128)(2,1)S(1)}, bf16[1552,768]{1,0:T(8,128)(2,1)}, u32[]{:S(2)}, u32[]{:S(2)}) %collective-permute-start.4) | collective-permute-done | bytes 2383904 | tf_op jit(solution)/shard_map/ppermute | solution.py:485
  71.3 3.1 copy.286
  74.5 4.0 %collective-permute-done.3.x_other = bf16[1,256,768]{2,1,0:T(8,128)(2,1)} collective-permute-done((bf16[1,256,768]{2,1,0:T(8,128)(2,1)}, bf16[1,256,768]{2,1,0:T(8,128)(2,1)}, u32[]{:S(2)}, u32[]{:S(2)}) %collective-permute-start.3) | collective-permute-done | bytes 393248 | tf_op jit(solution)/shard_map/ppermute | solution.py:485
  81.1 6.8 %mix_rows.4 = (bf16[4,512,768]{2,1,0:T(8,128)(2,1)S(1)}, bf16[4,512,768]{2,1,0:T(8,128)(2,1)}, f32[4,256,768]{2,1,0:T(8,128)}, f32[4,256,768]{2,1,0:T(8,128)}, f...) custom-call(s32[3]{0:T(128)S(1)} %pad_add_fusion.offs, ...), custom_call_target="tpu_custom_call" | custom-call | flops 2315255808 | bytes 10485760 | tf_op jit(solution)/shard_map/mix_rows/pallas_call | solution.py:109
  87.8 6.4 %mix_rows.5 = (bf16[4,512,768]{2,1,0:T(8,128)(2,1)S(1)}, bf16[4,512,768]{2,1,0:T(8,128)(2,1)}, f32[4,256,768]{2,1,0:T(8,128)}, f32[4,256,768]{2,1,0:T(8,128)}, f...) custom-call(s32[3]{0:T(128)S(1)} %pad_add_fusion.offs, ...), custom_call_target="tpu_custom_call", output_to_operand_aliasing={{0}: (14, {}), {1}: (15, {}), {2}: (16, {}), {3}: (17, {}),... | custom-call | flops 2315255808 | bytes 10485760 | tf_op jit(solution)/shard_map/mix_rows/pallas_call | solution.py:109
  94.2 7.0 %mix_rows.6 = (bf16[4,512,768]{2,1,0:T(8,128)(2,1)S(1)}, bf16[4,512,768]{2,1,0:T(8,128)(2,1)}, f32[4,256,768]{2,1,0:T(8,128)}, f32[4,256,768]{2,1,0:T(8,128)}, f...) custom-call(s32[3]{0:T(128)S(1)} %pad_add_fusion.offs, ...), custom_call_target="tpu_custom_call", output_to_operand_aliasing={{0}: (14, {}), {1}: (15, {}), {2}: (16, {}), {3}: (17, {}),... | custom-call | flops 2315255808 | bytes 10485760 | tf_op jit(solution)/shard_map/mix_rows/pallas_call | solution.py:109
  101.2 6.4 %mix_rows.7 = (bf16[4,512,768]{2,1,0:T(8,128)(2,1)S(1)}, bf16[4,512,768]{2,1,0:T(8,128)(2,1)}, f32[4,256,768]{2,1,0:T(8,128)}, f32[4,256,768]{2,1,0:T(8,128)}, f...) custom-call(s32[3]{0:T(128)S(1)} %pad_add_fusion.offs, ...), custom_call_target="tpu_custom_call", output_to_operand_aliasing={{0}: (14, {}), {1}: (15, {}), {2}: (16, {}), {3}: (17, {}),... | custom-call | flops 2315255808 | bytes 10485760 | tf_op jit(solution)/shard_map/mix_rows/pallas_call | solution.py:109
  107.6 1.6 copy-done.15
  111.5 24.1 %own_hidden.1 = (f32[1024,768]{1,0:T(8,128)}, f32[1024,768]{1,0:T(8,128)}, bf16[2,768,768]{2,1,0:T(8,128)(2,1)}, bf16[2,768,768]{2,1,0:T(8,128)(2,1)}, f32[1,768]{1,0:T(1,128)}, /*index=5*/f32[1,768]{1,0:T(1,128)}) custom-call(s32[1]{0:T(128)} %bitcast.2.core, bf16[1024,768]{1,0:T(8,128)(2,1)} %bitcast.166, bf16[1024,768]{1,0:T(8,128)(2,1)} %bitcast.185, ...), custom_call_target="tpu_custom_call" | custom-call | flops 14495514624 | bytes 25165824 | tf_op jit(solution)/shard_map/own_hidden/pallas_call | solution.py:207
  137.9 26.6 %other_hidden.1 = (f32[1024,768]{1,0:T(8,128)}, f32[1024,768]{1,0:T(8,128)}, bf16[2,768,768]{2,1,0:T(8,128)(2,1)}, bf16[2,768,768]{2,1,0:T(8,128)(2,1)}, f32[1,768]{1,0:T(1,128)}, /*index=5*/f32[1,768]{1,0:T(1,128)}) custom-call(bf16[1024,768]{1,0:T(8,128)(2,1)} %bitcast.167, bf16[1024,768]{1,0:T(8,128)(2,1)} %bitcast.186, bf16[768,1024]{1,0:T(8,128)(2,1)} %copy-done.19, ...), custom_call_target="tpu_custom_call" | custom-call | flops 14495514624 | bytes 25165824 | tf_op jit(solution)/shard_map/other_hidden/pallas_call | solution.py:237
  164.5 7.5 %back_rows.4 = (bf16[4,256,768]{2,1,0:T(8,128)(2,1)}, f32[4,256,768]{2,1,0:T(8,128)}, bf16[4,256,768]{2,1,0:T(8,128)(2,1)S(1)}, bf16[4,512,768]{2,1,0:T(8,128)(2...) custom-call(s32[3]{0:T(128)S(1)} %pad_add_fusion.offs, ...), custom_call_target="tpu_custom_call" | custom-call | flops 4000000000 | bytes 14680064 | tf_op jit(solution)/shard_map/back_rows/pallas_call | solution.py:319
  173.1 7.4 %back_rows.5 = (bf16[4,256,768]{2,1,0:T(8,128)(2,1)}, f32[4,256,768]{2,1,0:T(8,128)}, bf16[4,256,768]{2,1,0:T(8,128)(2,1)}, bf16[4,512,768]{2,1,0:T(8,128)(2,1)}...) custom-call(s32[3]{0:T(128)S(1)} %pad_add_fusion.offs, ...), custom_call_target="tpu_custom_call", output_to_operand_aliasing={{0}: (16, {}), {1}: (17, {}), {2}: (18, {}), {3}: (19, {}),... | custom-call | flops 4000000000 | bytes 14680064 | tf_op jit(solution)/shard_map/back_rows/pallas_call | solution.py:319
  180.6 7.6 %back_rows.6 = (bf16[4,256,768]{2,1,0:T(8,128)(2,1)}, f32[4,256,768]{2,1,0:T(8,128)}, bf16[4,256,768]{2,1,0:T(8,128)(2,1)}, bf16[4,512,768]{2,1,0:T(8,128)(2,1)}...) custom-call(s32[3]{0:T(128)S(1)} %pad_add_fusion.offs, ...), custom_call_target="tpu_custom_call", output_to_operand_aliasing={{0}: (16, {}), {1}: (17, {}), {2}: (18, {}), {3}: (19, {}),... | custom-call | flops 4000000000 | bytes 14680064 | tf_op jit(solution)/shard_map/back_rows/pallas_call | solution.py:319
  190.9 7.7 %back_rows.7 = (bf16[4,256,768]{2,1,0:T(8,128)(2,1)}, f32[4,256,768]{2,1,0:T(8,128)}, bf16[4,256,768]{2,1,0:T(8,128)(2,1)}, bf16[4,512,768]{2,1,0:T(8,128)(2,1)}...) custom-call(s32[3]{0:T(128)S(1)} %copy-done.35, ...), custom_call_target="tpu_custom_call", output_to_operand_aliasing={{0}: (16, {}), {1}: (17, {}), {2}: (18, {}), {3}: (19, {}),... | custom-call | flops 4000000000 | bytes 14680064 | tf_op jit(solution)/shard_map/back_rows/pallas_call | solution.py:319
  206.5 9.2 %square_grads.1 = (bf16[768,896]{1,0:T(8,128)(2,1)}, bf16[768,896]{1,0:T(8,128)(2,1)S(1)}) custom-call(s32[1]{0:T(128)} %bitcast.2.core, f32[1024,768]{1,0:T(8,128)S(1)} %bitcast.163, f32[1024,768]{1,0:T(8,128)} %bitcast.164, bf16[2048,768]{1,0:T(8,128)(2,1)} %bitcast.165, bf16[2048,768]{1,0:T(8,128)(2,1)} %bitcast.187, bf16[768,128]{1,0:T(8,128)(2,1)S(1)} %fusion.20.vectors), custom_call_target="tpu_custom_call" | custom-call | flops 3623878656 | bytes 16777216 | tf_op jit(solution)/shard_map/square_grads/pallas_call | solution.py:438
  217.3 3.1 fusion
  220.4 1.8 collective-permute-start.22
  222.2 2.3 fusion.6
  226.3 10.4 %logits_grad.1 = (bf16[6,512,256]{2,1,0:T(8,128)(2,1)}, bf16[6,512,256]{2,1,0:T(8,128)(2,1)S(1)}) custom-call(s32[3]{0:T(128)S(1)} %copy-done.36, bf16[4,256,768]{2,1,0:T(8,128)(2,1)S(1)} %copy-done.17, f32[4,256,768]{2,1,0:T(8,128)S(1)} %copy-done.2, bf16[4,512,768]{2,1,0:T(8,128)(2,1)S(1)} %copy-done.14, s32[4,512,1]{2,1,0:T(8,128)S(1)} %copy-done.7, ...), custom_call_target="tpu_custom_call" | custom-call | flops 3221225472 | bytes 16777216 | tf_op jit(solution)/shard_map/logits_grad/pallas_call | solution.py:392
  237.8 11.7 %collective-permute-done.22 = bf16[2,2,2,2,48,768]{5,4,0,3,2,1:T(8,128)(2,1)} collective-permute-done((bf16[2,2,2,2,48,768]{5,4,0,3,2,1:T(8,128)(2,1)}, bf16[2,2,2,2,48,768]{5,4,0,3,2,1:T(8,128)(2,1)}, u32[]{:S(2)}, u32[]{:S(2)}) %collective-permute-start.22) | collective-permute-done | bytes 1179680 | tf_op jit(solution)/shard_map/ppermute | solution.py:485
  249.5 2.5 fusion.3
  252.0 1.8 collective-permute-start.23
  255.3 8.5 %collective-permute-done.11 = bf16[2,2,2,2,24,896]{5,4,2,3,1,0:T(8,128)(2,1)} collective-permute-done((bf16[2,2,2,2,24,896]{5,4,2,3,1,0:T(8,128)(2,1)}, bf16[2,2,2,2,24,896]{5,4,2,3,1,0:T(8,128)(2,1)}, u32[]{:S(2)}, u32[]{:S(2)}) %collective-permute-start.11) | collective-permute-done | bytes 688160 | tf_op jit(solution)/shard_map/ppermute | solution.py:485
  263.9 1.7 collective-permute-start.8
  269.7 2.1 fusion.1
  271.8 1.8 collective-permute-start.6
  275.9 1.7 collective-permute-start.26
  277.6 2.0 fusion.11
  284.5 2.6 collective-permute-start.24
  288.6 2.9 collective-permute-done.6.gh_received
  294.0 2.9 collective-permute-start.13
  299.9 1.8 constant_dynamic-slice_fusion.17
  301.7 4.0 %collective-permute-done.13 = bf16[2,2,24,896]{3,2,0,1:T(8,128)(2,1)S(1)} collective-permute-done((bf16[2,2,24,896]{3,2,0,1:T(8,128)(2,1)S(1)}, bf16[2,2,24,896]{3,2,0,1:T(8,128)(2,1)S(1)}, u32[]{:S(2)}, u32[]{:S(2)}) %collective-permute-start.13) | collective-permute-done | bytes 172064 | tf_op jit(solution)/shard_map/ppermute | solution.py:485
  309.4 1.9 collective-permute-done.14
  312.3 1.9 fusion.2
  315.0 3.5 collective-permute-done.17
  318.5 2.2 fusion.5
  322.8 10.9 %collective-permute-done.27 = bf16[2,2,2,48,768]{4,3,0,2,1:T(8,128)(2,1)S(1)} collective-permute-done((bf16[2,2,2,48,768]{4,3,0,2,1:T(8,128)(2,1)S(1)}, bf16[2,2,2,48,768]{4,3,0,2,1:T(8,128)(2,1)S(1)}, u32[]{:S(2)}, u32[]{:S(2)}) %collective-permute-start.27) | collective-permute-done | bytes 589856 | tf_op jit(solution)/shard_map/ppermute | solution.py:485
  336.1 3.8 %collective-permute-done.18 = bf16[6,2,2,32,256]{4,3,0,2,1:T(8,128)(2,1)} collective-permute-done((bf16[6,2,2,32,256]{4,3,0,2,1:T(8,128)(2,1)}, bf16[6,2,2,32,256]{4,3,0,2,1:T(8,128)(2,1)}, u32[]{:S(2)}, u32[]{:S(2)}) %collective-permute-start.18) | collective-permute-done | bytes 393248 | tf_op jit(solution)/shard_map/ppermute | solution.py:485
  341.1 2.0 collective-permute-start.19
  343.1 10.2 %collective-permute-done.28 = bf16[2,2,48,768]{3,2,0,1:T(8,128)(2,1)S(1)} collective-permute-done((bf16[2,2,48,768]{3,2,0,1:T(8,128)(2,1)S(1)}, bf16[2,2,48,768]{3,2,0,1:T(8,128)(2,1)S(1)}, u32[]{:S(2)}, u32[]{:S(2)}) %collective-permute-start.28) | collective-permute-done | bytes 294944 | tf_op jit(solution)/shard_map/ppermute | solution.py:485
  358.7 2.6 collective-permute-done.29
  (215 shorter events, 66.5 us)
Async XLA Ops:
  3.2 12.1 %collective-permute-start.2 = (bf16[1,256,768]{2,1,0:T(8,128)(2,1)S(1)}, bf16[1,256,768]{2,1,0:T(8,128)(2,1)S(1)}, u32[]{:S(2)}, u32[]{:S(2)}) collective-permute-start(bf16[1,256,768]{2,1,0:T(8,128)(2,1)S(1)} %get-tuple-element.191), channel_id=1, source_target_pairs={{0,1},{1,0},{2,3},{3,2},{4,5},{5,4},{6,7},{7,6},{8,9},{9,8},{10,11... | collective-permute-start | bytes 1179656 | tf_op jit(solution)/shard_map/ppermute | solution.py:485
  15.3 54.8 %collective-permute-start.4 = (bf16[1552,768]{1,0:T(8,128)(2,1)S(1)}, bf16[1552,768]{1,0:T(8,128)(2,1)}, u32[]{:S(2)}, u32[]{:S(2)}) collective-permute-start(bf16[1552,768]{1,0:T(8,128)(2,1)S(1)} %pad_maximum_fusion), channel_id=1, source_target_pairs={{0,1},{1,0},{2,3},{3,2},{4,5},{5,4},{6,7},{7,6},{8,9},{9,8},{10,11... | collective-permute-start | bytes 7151624 | tf_op jit(solution)/shard_map/ppermute | solution.py:485
  17.0 61.5 %collective-permute-start.3 = (bf16[1,256,768]{2,1,0:T(8,128)(2,1)}, bf16[1,256,768]{2,1,0:T(8,128)(2,1)}, u32[]{:S(2)}, u32[]{:S(2)}) collective-permute-start(bf16[1,256,768]{2,1,0:T(8,128)(2,1)} %get-tuple-element.190), channel_id=1, source_target_pairs={{0,1},{1,0},{2,3},{3,2},{4,5},{5,4},{6,7},{7,6},{8,9},{9,8},{10,11... | collective-permute-start | bytes 1179656 | tf_op jit(solution)/shard_map/ppermute | solution.py:485
  17.3 76.9 %collective-permute-start.1 = (bf16[1,256,768]{2,1,0:T(8,128)(2,1)}, bf16[1,256,768]{2,1,0:T(8,128)(2,1)}, u32[]{:S(2)}, u32[]{:S(2)}) collective-permute-start(bf16[1,256,768]{2,1,0:T(8,128)(2,1)} %get-tuple-element.192), channel_id=1, source_target_pairs={{0,1},{1,0},{2,3},{3,2},{4,5},{5,4},{6,7},{7,6},{8,9},{9,8},{10,11... | collective-permute-start | bytes 1179656 | tf_op jit(solution)/shard_map/ppermute | solution.py:485
  19.0 82.2 %collective-permute-start = (bf16[1,256,768]{2,1,0:T(8,128)(2,1)}, bf16[1,256,768]{2,1,0:T(8,128)(2,1)S(1)}, u32[]{:S(2)}, u32[]{:S(2)}) collective-permute-start(bf16[1,256,768]{2,1,0:T(8,128)(2,1)} %get-tuple-element.193), channel_id=1, source_target_pairs={{0,1},{1,0},{2,3},{3,2},{4,5},{5,4},{6,7},{7,6},{8,9},{9,8},{10,11... | collective-permute-start | bytes 1179656 | tf_op jit(solution)/shard_map/ppermute | solution.py:485
  19.3 51.4 %copy-start.46 = (s32[4,512]{1,0:T(4,128)S(1)}, s32[4,512]{1,0:T(4,128)}, u32[]{:S(2)}) copy-start(s32[4,512]{1,0:T(4,128)} %param.17) | copy-start | bytes 24580
  19.3 51.8 %copy-start.48 = (bf16[768]{0:T(1024)(128)(2,1)S(1)}, bf16[768]{0:T(1024)(128)(2,1)}, u32[]{:S(2)}) copy-start(bf16[768]{0:T(1024)(128)(2,1)} %param.18) | copy-start | bytes 4612
  19.3 51.9 %copy-start.49 = (bf16[768]{0:T(1024)(128)(2,1)S(1)}, bf16[768]{0:T(1024)(128)(2,1)}, u32[]{:S(2)}) copy-start(bf16[768]{0:T(1024)(128)(2,1)} %param.25) | copy-start | bytes 4612
  19.3 51.9 %copy-start.50 = (bf16[768]{0:T(1024)(128)(2,1)S(1)}, bf16[768]{0:T(1024)(128)(2,1)}, u32[]{:S(2)}) copy-start(bf16[768]{0:T(1024)(128)(2,1)} %param.21) | copy-start | bytes 4612
  19.3 51.9 %copy-start.51 = (bf16[768]{0:T(1024)(128)(2,1)S(1)}, bf16[768]{0:T(1024)(128)(2,1)}, u32[]{:S(2)}) copy-start(bf16[768]{0:T(1024)(128)(2,1)} %param.24) | copy-start | bytes 4612
  19.3 51.9 %copy-start.52 = (bf16[768]{0:T(1024)(128)(2,1)S(1)}, bf16[768]{0:T(1024)(128)(2,1)}, u32[]{:S(2)}) copy-start(bf16[768]{0:T(1024)(128)(2,1)} %param.19) | copy-start | bytes 4612
  19.4 51.9 %copy-start.53 = (bf16[768]{0:T(1024)(128)(2,1)S(1)}, bf16[768]{0:T(1024)(128)(2,1)}, u32[]{:S(2)}) copy-start(bf16[768]{0:T(1024)(128)(2,1)} %param.26) | copy-start | bytes 4612
  70.1 67.8 %collective-permute-start.5 = (bf16[1552,768]{1,0:T(8,128)(2,1)}, bf16[1552,768]{1,0:T(8,128)(2,1)}, u32[]{:S(2)}, u32[]{:S(2)}) collective-permute-start(bf16[1552,768]{1,0:T(8,128)(2,1)} %collective-permute-done.4.w_mine), channel_id=1, source_target_pairs={{0,2},{2,0},{4,6},{6,4},{8,10},{10,8},{12,14},{14,12},{16,18},{18,... | collective-permute-start | bytes 7151624 | tf_op jit(solution)/shard_map/ppermute | solution.py:485
  70.2 110.4 %copy-start.34 = (s32[3]{0:T(128)}, s32[3]{0:T(128)S(1)}, u32[]{:S(2)}) copy-start(s32[3]{0:T(128)S(1)} %pad_add_fusion.offs) | copy-start | bytes 40
  71.2 109.4 %copy-start.5 = (s32[4,512,1]{2,1,0:T(8,128)}, s32[4,512,1]{2,1,0:T(8,128)S(1)}, u32[]{:S(2)}) copy-start(s32[4,512,1]{2,1,0:T(8,128)S(1)} %copy.234.seg_col) | copy-start | bytes 24580
  74.5 106.1 %copy-start.32 = (f32[1,768]{1,0:T(1,128)}, f32[1,768]{1,0:T(1,128)S(1)}, u32[]{:S(2)}) copy-start(f32[1,768]{1,0:T(1,128)S(1)} %reshape.519.bd) | copy-start | bytes 9220
  135.6 81.7 %collective-permute-start.21 = (bf16[2,768,768]{2,1,0:T(8,128)(2,1)}, bf16[2,768,768]{2,1,0:T(8,128)(2,1)}, u32[]{:S(2)}, u32[]{:S(2)}) collective-permute-start(bf16[2,768,768]{2,1,0:T(8,128)(2,1)} %get-tuple-element.166), channel_id=1, source_target_pairs={{0,2},{2,0},{4,6},{6,4},{8,10},{10,8},{12,14},{14,12},{16,18},{18,... | collective-permute-start | bytes 7077896 | tf_op jit(solution)/shard_map/ppermute | solution.py:485
  137.9 26.6 %copy-start.10 = (bf16[768,768]{1,0:T(8,128)(2,1)S(1)}, bf16[768,768]{1,0:T(8,128)(2,1)}, u32[]{:S(2)}) copy-start(bf16[768,768]{1,0:T(8,128)(2,1)} %wv.15) | copy-start | bytes 3538948
  137.9 26.6 %copy-start.13 = (bf16[768,768]{1,0:T(8,128)(2,1)S(1)}, bf16[768,768]{1,0:T(8,128)(2,1)}, u32[]{:S(2)}) copy-start(bf16[768,768]{1,0:T(8,128)(2,1)} %wo.15) | copy-start | bytes 3538948
  216.8 5.4 %collective-permute-start.10 = (bf16[768,896]{1,0:T(8,128)(2,1)}, bf16[768,896]{1,0:T(8,128)(2,1)}, u32[]{:S(2)}, u32[]{:S(2)}) collective-permute-start(bf16[768,896]{1,0:T(8,128)(2,1)} %get-tuple-element.160), channel_id=1, source_target_pairs={{0,2},{2,0},{4,6},{6,4},{8,10},{10,8},{12,14},{14,12},{16,18},{18,... | collective-permute-start | bytes 4128776 | tf_op jit(solution)/shard_map/ppermute | solution.py:485
  217.3 52.0 %collective-permute-start.25 = (bf16[2,768,768]{2,1,0:T(8,128)(2,1)}, bf16[2,768,768]{2,1,0:T(8,128)(2,1)}, u32[]{:S(2)}, u32[]{:S(2)}) collective-permute-start(bf16[2,768,768]{2,1,0:T(8,128)(2,1)} %get-tuple-element.168), channel_id=1, source_target_pairs={{0,2},{2,0},{4,6},{6,4},{8,10},{10,8},{12,14},{14,12},{16,18},{18,... | collective-permute-start | bytes 7077896 | tf_op jit(solution)/shard_map/ppermute | solution.py:485
  220.4 29.1 %collective-permute-start.22 = (bf16[2,2,2,2,48,768]{5,4,0,3,2,1:T(8,128)(2,1)}, bf16[2,2,2,2,48,768]{5,4,0,3,2,1:T(8,128)(2,1)}, u32[]{:S(2)}, u32[]{:S(2)}) collective-permute-start(bf16[2,2,2,2,48,768]{5,4,0,3,2,1:T(8,128)(2,1)} %fusion), channel_id=1, source_target_pairs={{0,4},{2,6},{4,0},{6,2},{8,12},{10,14},{12,8},{14,10},{16,20},{18,... | collective-permute-start | bytes 3538952 | tf_op jit(solution)/shard_map/ppermute | solution.py:485
  224.5 39.3 %collective-permute-start.11 = (bf16[2,2,2,2,24,896]{5,4,2,3,1,0:T(8,128)(2,1)}, bf16[2,2,2,2,24,896]{5,4,2,3,1,0:T(8,128)(2,1)}, u32[]{:S(2)}, u32[]{:S(2)}) collective-permute-start(bf16[2,2,2,2,24,896]{5,4,2,3,1,0:T(8,128)(2,1)} %fusion.6), channel_id=1, source_target_pairs={{0,4},{2,6},{4,0},{6,2},{8,12},{10,14},{12,8},{14,10},{16,20},{18,... | collective-permute-start | bytes 2064392 | tf_op jit(solution)/shard_map/ppermute | solution.py:485
  237.8 26.0 %copy-start.31 = (bf16[1,256,768]{2,1,0:T(8,128)(2,1)S(1)}, bf16[1,256,768]{2,1,0:T(8,128)(2,1)}, u32[]{:S(2)}) copy-start(bf16[1,256,768]{2,1,0:T(8,128)(2,1)} %copy-done.30) | copy-start | bytes 1179652
  237.8 59.1 %collective-permute-start.16 = (bf16[6,512,256]{2,1,0:T(8,128)(2,1)}, bf16[6,512,256]{2,1,0:T(8,128)(2,1)}, u32[]{:S(2)}, u32[]{:S(2)}) collective-permute-start(bf16[6,512,256]{2,1,0:T(8,128)(2,1)} %get-tuple-element.164), channel_id=1, source_target_pairs={{0,2},{2,0},{4,6},{6,4},{8,10},{10,8},{12,14},{14,12},{16,18},{18,... | collective-permute-start | bytes 4718600 | tf_op jit(solution)/shard_map/ppermute | solution.py:485
  249.5 22.3 %copy-start.38 = (bf16[1,256,768]{2,1,0:T(8,128)(2,1)S(1)}, bf16[1,256,768]{2,1,0:T(8,128)(2,1)}, u32[]{:S(2)}) copy-start(bf16[1,256,768]{2,1,0:T(8,128)(2,1)} %copy-done.37) | copy-start | bytes 1179652
  252.0 19.7 %collective-permute-start.23 = (bf16[2,2,2,48,768]{4,3,0,2,1:T(8,128)(2,1)}, bf16[2,2,2,48,768]{4,3,0,2,1:T(8,128)(2,1)}, u32[]{:S(2)}, u32[]{:S(2)}) collective-permute-start(bf16[2,2,2,48,768]{4,3,0,2,1:T(8,128)(2,1)} %fusion.3), channel_id=1, source_target_pairs={{0,8},{2,10},{4,12},{6,14},{8,0},{10,2},{12,4},{14,6},{16,24},{18,... | collective-permute-start | bytes 1769480 | tf_op jit(solution)/shard_map/ppermute | solution.py:485
  253.8 19.7 %collective-permute-start.9 = (bf16[1,256,768]{2,1,0:T(8,128)(2,1)S(1)}, bf16[1,256,768]{2,1,0:T(8,128)(2,1)S(1)}, u32[]{:S(2)}, u32[]{:S(2)}) collective-permute-start(bf16[1,256,768]{2,1,0:T(8,128)(2,1)S(1)} %copy-done.29), channel_id=1, source_target_pairs={{0,1},{1,0},{2,3},{3,2},{4,5},{5,4},{6,7},{7,6},{8,9},{9,8},{10,11... | collective-permute-start | bytes 1179656 | tf_op jit(solution)/shard_map/ppermute | solution.py:485
  263.9 12.0 %collective-permute-start.8 = (bf16[1,256,768]{2,1,0:T(8,128)(2,1)S(1)}, bf16[1,256,768]{2,1,0:T(8,128)(2,1)S(1)}, u32[]{:S(2)}, u32[]{:S(2)}) collective-permute-start(bf16[1,256,768]{2,1,0:T(8,128)(2,1)S(1)} %copy-done.31), channel_id=1, source_target_pairs={{0,1},{1,0},{2,3},{3,2},{4,5},{5,4},{6,7},{7,6},{8,9},{9,8},{10,11... | collective-permute-start | bytes 1179656 | tf_op jit(solution)/shard_map/ppermute | solution.py:485
  269.3 15.2 %collective-permute-start.7 = (bf16[1,256,768]{2,1,0:T(8,128)(2,1)S(1)}, bf16[1,256,768]{2,1,0:T(8,128)(2,1)S(1)}, u32[]{:S(2)}, u32[]{:S(2)}) collective-permute-start(bf16[1,256,768]{2,1,0:T(8,128)(2,1)S(1)} %copy-done.27), channel_id=1, source_target_pairs={{0,1},{1,0},{2,3},{3,2},{4,5},{5,4},{6,7},{7,6},{8,9},{9,8},{10,11... | collective-permute-start | bytes 1179656 | tf_op jit(solution)/shard_map/ppermute | solution.py:485
  271.8 19.7 %collective-permute-start.6 = (bf16[1,256,768]{2,1,0:T(8,128)(2,1)S(1)}, bf16[1,256,768]{2,1,0:T(8,128)(2,1)S(1)}, u32[]{:S(2)}, u32[]{:S(2)}) collective-permute-start(bf16[1,256,768]{2,1,0:T(8,128)(2,1)S(1)} %copy-done.38), channel_id=1, source_target_pairs={{0,1},{1,0},{2,3},{3,2},{4,5},{5,4},{6,7},{7,6},{8,9},{9,8},{10,11... | collective-permute-start | bytes 1179656 | tf_op jit(solution)/shard_map/ppermute | solution.py:485
  273.6 19.4 %collective-permute-start.12 = (bf16[2,2,2,24,896]{4,3,1,2,0:T(8,128)(2,1)S(1)}, bf16[2,2,2,24,896]{4,3,1,2,0:T(8,128)(2,1)S(1)}, u32[]{:S(2)}, u32[]{:S(2)}) collective-permute-start(bf16[2,2,2,24,896]{4,3,1,2,0:T(8,128)(2,1)S(1)} %fusion.7), channel_id=1, source_target_pairs={{0,8},{2,10},{4,12},{6,14},{8,0},{10,2},{12,4},{14,6},{16,24},{18,... | collective-permute-start | bytes 1032200 | tf_op jit(solution)/shard_map/ppermute | solution.py:485
  275.9 36.4 %collective-permute-start.26 = (bf16[2,2,2,2,48,768]{5,4,0,3,2,1:T(8,128)(2,1)S(1)}, bf16[2,2,2,2,48,768]{5,4,0,3,2,1:T(8,128)(2,1)S(1)}, u32[]{:S(2)}, u32[]{:S(2)}) collective-permute-start(bf16[2,2,2,2,48,768]{5,4,0,3,2,1:T(8,128)(2,1)S(1)} %fusion.1), channel_id=1, source_target_pairs={{0,4},{2,6},{4,0},{6,2},{8,12},{10,14},{12,8},{14,10},{16,20},{18,... | collective-permute-start | bytes 3538952 | tf_op jit(solution)/shard_map/ppermute | solution.py:485
  284.5 74.2 %collective-permute-start.24 = (bf16[2,2,48,768]{3,2,0,1:T(8,128)(2,1)}, bf16[2,2,48,768]{3,2,0,1:T(8,128)(2,1)}, u32[]{:S(2)}, u32[]{:S(2)}) collective-permute-start(bf16[2,2,48,768]{3,2,0,1:T(8,128)(2,1)} %fusion.11), channel_id=1, source_target_pairs={{0,16},{2,18},{4,20},{6,22},{8,24},{10,26},{12,28},{14,30},{16,0},... | collective-permute-start | bytes 884744 | tf_op jit(solution)/shard_map/ppermute | solution.py:485
  294.0 11.7 %collective-permute-start.13 = (bf16[2,2,24,896]{3,2,0,1:T(8,128)(2,1)S(1)}, bf16[2,2,24,896]{3,2,0,1:T(8,128)(2,1)S(1)}, u32[]{:S(2)}, u32[]{:S(2)}) collective-permute-start(bf16[2,2,24,896]{3,2,0,1:T(8,128)(2,1)S(1)} %fusion.19), channel_id=1, source_target_pairs={{0,16},{2,18},{4,20},{6,22},{8,24},{10,26},{12,28},{14,30},{16,0},... | collective-permute-start | bytes 516104 | tf_op jit(solution)/shard_map/ppermute | solution.py:485
  298.3 20.1 %collective-permute-start.17 = (bf16[6,2,2,2,32,256]{5,4,0,3,2,1:T(8,128)(2,1)S(1)}, bf16[6,2,2,2,32,256]{5,4,0,3,2,1:T(8,128)(2,1)S(1)}, u32[]{:S(2)}, u32[]{:S(2)}) collective-permute-start(bf16[6,2,2,2,32,256]{5,4,0,3,2,1:T(8,128)(2,1)S(1)} %fusion.4), channel_id=1, source_target_pairs={{0,4},{2,6},{4,0},{6,2},{8,12},{10,14},{12,8},{14,10},{16,20},{18,... | collective-permute-start | bytes 2359304 | tf_op jit(solution)/shard_map/ppermute | solution.py:485
  306.7 4.6 %collective-permute-start.14 = (bf16[2,24,896]{2,1,0:T(8,128)(2,1)S(1)}, bf16[2,24,896]{2,1,0:T(8,128)(2,1)S(1)}, u32[]{:S(2)}, u32[]{:S(2)}) collective-permute-start(bf16[2,24,896]{2,1,0:T(8,128)(2,1)S(1)} %fusion.21), channel_id=1, source_target_pairs={{0,1},{1,0},{2,3},{3,2},{4,5},{5,4},{6,7},{7,6},{8,9},{9,8},{10,11... | collective-permute-start | bytes 258056 | tf_op jit(solution)/shard_map/ppermute | solution.py:485
  312.3 21.4 %copy-start.39 = (bf16[2,2,2,2,48,768]{5,4,0,3,2,1:T(8,128)(2,1)}, bf16[2,2,2,2,48,768]{5,4,0,3,2,1:T(8,128)(2,1)S(1)}, u32[]{:S(2)}) copy-start(bf16[2,2,2,2,48,768]{5,4,0,3,2,1:T(8,128)(2,1)S(1)} %collective-permute-done.26) | copy-start | bytes 3538948
  314.2 19.5 %collective-permute-start.27 = (bf16[2,2,2,48,768]{4,3,0,2,1:T(8,128)(2,1)S(1)}, bf16[2,2,2,48,768]{4,3,0,2,1:T(8,128)(2,1)S(1)}, u32[]{:S(2)}, u32[]{:S(2)}) collective-permute-start(bf16[2,2,2,48,768]{4,3,0,2,1:T(8,128)(2,1)S(1)} %fusion.2), channel_id=1, source_target_pairs={{0,8},{2,10},{4,12},{6,14},{8,0},{10,2},{12,4},{14,6},{16,24},{18,... | collective-permute-start | bytes 1769480 | tf_op jit(solution)/shard_map/ppermute | solution.py:485
  315.0 7.1 %collective-permute-start.15 = (bf16[24,896]{1,0:T(8,128)(2,1)S(1)}, bf16[24,896]{1,0:T(8,128)(2,1)S(1)}, u32[]{:S(2)}, u32[]{:S(2)}) collective-permute-start(bf16[24,896]{1,0:T(8,128)(2,1)S(1)} %fusion.25), channel_id=1, source_target_pairs={{0,2},{2,0},{4,6},{6,4},{8,10},{10,8},{12,14},{14,12},{16,18},{18,... | collective-permute-start | bytes 129032 | tf_op jit(solution)/shard_map/ppermute | solution.py:485
  320.7 19.3 %collective-permute-start.18 = (bf16[6,2,2,32,256]{4,3,0,2,1:T(8,128)(2,1)}, bf16[6,2,2,32,256]{4,3,0,2,1:T(8,128)(2,1)}, u32[]{:S(2)}, u32[]{:S(2)}) collective-permute-start(bf16[6,2,2,32,256]{4,3,0,2,1:T(8,128)(2,1)} %fusion.5), channel_id=1, source_target_pairs={{0,8},{2,10},{4,12},{6,14},{8,0},{10,2},{12,4},{14,6},{16,24},{18,... | collective-permute-start | bytes 1179656 | tf_op jit(solution)/shard_map/ppermute | solution.py:485
  333.9 22.2 %copy-start.43 = (bf16[6,1,1,1,2,32,256]{6,5,4,3,2,1,0:T(8,128)(2,1)S(1)}, bf16[6,1,1,1,2,32,256]{6,5,4,3,2,1,0:T(8,128)(2,1)}, u32[]{:S(2)}) copy-start(bf16[6,1,1,1,2,32,256]{6,5,4,3,2,1,0:T(8,128)(2,1)} %get-tuple-element.186) | copy-start | bytes 589828
  333.9 22.2 %copy-start.44 = (bf16[6,1,1,1,2,32,256]{6,5,4,3,2,1,0:T(8,128)(2,1)S(1)}, bf16[6,1,1,1,2,32,256]{6,5,4,3,2,1,0:T(8,128)(2,1)}, u32[]{:S(2)}) copy-start(bf16[6,1,1,1,2,32,256]{6,5,4,3,2,1,0:T(8,128)(2,1)} %get-tuple-element.188) | copy-start | bytes 589828
  333.9 19.4 %collective-permute-start.28 = (bf16[2,2,48,768]{3,2,0,1:T(8,128)(2,1)S(1)}, bf16[2,2,48,768]{3,2,0,1:T(8,128)(2,1)S(1)}, u32[]{:S(2)}, u32[]{:S(2)}) collective-permute-start(bf16[2,2,48,768]{3,2,0,1:T(8,128)(2,1)S(1)} %fusion.8), channel_id=1, source_target_pairs={{0,16},{2,18},{4,20},{6,22},{8,24},{10,26},{12,28},{14,30},{16,0},... | collective-permute-start | bytes 884744 | tf_op jit(solution)/shard_map/ppermute | solution.py:485
  341.1 15.0 %collective-permute-start.19 = (bf16[6,2,32,256]{3,2,0,1:T(8,128)(2,1)S(1)}, bf16[6,2,32,256]{3,2,0,1:T(8,128)(2,1)S(1)}, u32[]{:S(2)}, u32[]{:S(2)}) collective-permute-start(bf16[6,2,32,256]{3,2,0,1:T(8,128)(2,1)S(1)} %fusion.17), channel_id=1, source_target_pairs={{0,16},{2,18},{4,20},{6,22},{8,24},{10,26},{12,28},{14,30},{16,0},... | collective-permute-start | bytes 589832 | tf_op jit(solution)/shard_map/ppermute | solution.py:485
  354.5 6.8 %collective-permute-start.29 = (bf16[2,2,48,768]{3,2,0,1:T(8,128)(2,1)S(1)}, bf16[2,2,48,768]{3,2,0,1:T(8,128)(2,1)S(1)}, u32[]{:S(2)}, u32[]{:S(2)}) collective-permute-start(bf16[2,2,48,768]{3,2,0,1:T(8,128)(2,1)S(1)} %fusion.10), channel_id=1, source_target_pairs={{0,1},{1,0},{2,3},{3,2},{4,5},{5,4},{6,7},{7,6},{8,9},{9,8},{10,11... | collective-permute-start | bytes 884744 | tf_op jit(solution)/shard_map/ppermute | solution.py:485
  357.3 1.4 collective-permute-start.20
  362.6 1.4 collective-permute-start.30
  (38 other events, 256.6 us)
